TPU v7x, 32 devices: a whole 2x2x4 slice. The times are simulated.
32 devices in a mesh: dp: 4 (over y, x), rows: 8 (over z, core).
Axes of the slice: x: 2, y: 2, z: 4, core: 2. Of those that a mesh axis runs over, the one named last changes fastest.
Arguments:
- latents: bfloat16 [8, 512, 1024], P('dp'), may hold values from -6 to 6
- pixels: bfloat16 [8, 12544, 261], P('dp', 'rows'), may hold values from -6 to 6
- pix_counts: int32 [8], P('dp'), may hold values from 1024 to 12544, as said below
- cotangent: bfloat16 [8, 512, 1024], P('dp'), may hold values from -6 to 6
- weight_mats: float32 [10, 1024, 1024], P(None, ('dp', 'rows'))
- kv_weights: float32 [2, 261, 1024], P(None, None, ('dp', 'rows')), may hold values from -0.375 to 0.375
- norm_gains: float32 [4, 1024], P(None, ('dp', 'rows')), may hold values from 0.5 to 1.5
- input_gain: float32 [261], replicated, may hold values from 0.5 to 1.5
- mats_first: float32 [10, 1024, 1024], P(None, ('dp', 'rows'))
- mats_second: float32 [10, 1024, 1024], P(None, ('dp', 'rows')), may hold values from 1 to 100
- kv_first: float32 [2, 261, 1024], P(None, None, ('dp', 'rows')), may hold values from -6 to 6
- kv_second: float32 [2, 261, 1024], P(None, None, ('dp', 'rows')), may hold values from 1 to 100
- gains_first: float32 [4, 1024], P(None, ('dp', 'rows')), may hold values from -6 to 6
- gains_second: float32 [4, 1024], P(None, ('dp', 'rows')), may hold values from 1 to 100
- input_first: float32 [261], replicated, may hold values from -6 to 6
- input_second: float32 [261], replicated, may hold values from 1 to 100
Outputs:
- block_out: bfloat16 [8, 512, 1024], P('dp', 'rows')
- latent_grad: float32 [8, 512, 1024], P('dp', 'rows')
- pixel_grad: float32 [8, 12544, 261], P('dp', 'rows')
- mats_grad: float32 [10, 1024, 1024], P(None, ('dp', 'rows'))
- kv_grad: float32 [2, 261, 1024], P(None, None, ('dp', 'rows'))
- gains_grad: float32 [4, 1024], P(None, ('dp', 'rows'))
- input_grad: float32 [261], replicated
- mats_new: float32 [10, 1024, 1024], P(None, ('dp', 'rows'))
- mats_first_new: float32 [10, 1024, 1024], P(None, ('dp', 'rows'))
- mats_second_new: float32 [10, 1024, 1024], P(None, ('dp', 'rows'))
- kv_new: float32 [2, 261, 1024], P(None, None, ('dp', 'rows'))
- kv_first_new: float32 [2, 261, 1024], P(None, None, ('dp', 'rows'))
- kv_second_new: float32 [2, 261, 1024], P(None, None, ('dp', 'rows'))
- gains_new: float32 [4, 1024], P(None, ('dp', 'rows'))
- gains_first_new: float32 [4, 1024], P(None, ('dp', 'rows'))
- gains_second_new: float32 [4, 1024], P(None, ('dp', 'rows'))
- input_new: float32 [261], replicated
- input_first_new: float32 [261], replicated
- input_second_new: float32 [261], replicated
Inputs may be any that keep to these rules, and one draw needn't show every extreme that they name: The first pix_counts[i] pixel rows of item i are valid, the rest padding; in each group of 2 items on one index of dp, one item drawn from the seed has all 12544 rows valid.
All inputs are finite; a program needn't handle non-finite values.
Results may differ from a plain program's by a relative error of at most 0.025.
Values may be sent and summed in bfloat16 or wider, within the bound.
A program may use at most 320 MiB of HBM per device.

v0:
```python
import jax
import jax.numpy as jnp
from jax import lax
from jax.sharding import PartitionSpec as P

HEADS = 8


first_fix = 1.0 - 0.9**10
second_fix = 1.0 - 0.999**10
step_rate = 0.25
decay_rate = 0.01


def standard(values):
    centred = values - jnp.mean(values, -1, keepdims=True)
    return centred * lax.rsqrt(jnp.mean(centred * centred, -1, keepdims=True) + 1e-05)


def softmax_rows(scores):
    exp_scores = jnp.exp(scores - jnp.max(scores, -1, keepdims=True))
    return exp_scores / jnp.sum(exp_scores, -1, keepdims=True)


def product(left_side, right_side):
    return jnp.dot(left_side, right_side, preferred_element_type=jnp.float32)


def product_tn(left_side, right_side):
    return lax.dot_general(
        left_side, right_side, (((0,), (0,)), ((), ())), preferred_element_type=jnp.float32
    )


def product_nt(left_side, right_side):
    return lax.dot_general(
        left_side, right_side, (((1,), (1,)), ((), ())), preferred_element_type=jnp.float32
    )


def moments(weight, gradient, first_mom, second, sum_axes):
    first_new = 0.9 * first_mom + 0.1 * gradient
    second_new = 0.999 * second + 0.001 * gradient * gradient
    update = (
        first_new / first_fix / (jnp.sqrt(second_new / second_fix) + 1e-06) + decay_rate * weight
    )
    return (
        first_new,
        second_new,
        update,
        jnp.sum(weight * weight, sum_axes),
        jnp.sum(update * update, sum_axes),
    )


def local(
    latents,
    pixels,
    pix_counts,
    cotangent,
    weight_mats,
    kv_weights,
    norm_gains,
    input_gain,
    mats_first,
    mats_second,
    kv_first,
    kv_second,
    gains_first,
    gains_second,
    input_first,
    input_second,
):
    item_count, lat_len, model_width = latents.shape
    pix_dev = pixels.shape[1]
    row_count = lax.axis_size("rows")
    lat_share = lat_len // row_count
    row_rank = lax.axis_index("rows")
    head_dim = model_width // HEADS
    all_rows = item_count * lat_len
    bf_type = jnp.bfloat16
    fl_type = jnp.float32
    wide_weights = (
        weight_mats.astype(bf_type),
        kv_weights.astype(bf_type),
        norm_gains.astype(bf_type),
    )
    w_mats, w_pairs, w_gains = (
        lax.all_gather(wide_weights[0], ("dp", "rows"), axis=1, tiled=True),
        lax.all_gather(wide_weights[1], ("dp", "rows"), axis=2, tiled=True),
        lax.all_gather(wide_weights[2], ("dp", "rows"), axis=1, tiled=True),
    )
    gain_rows = w_gains.astype(fl_type)

    def own_rows(values):
        shaped = values.reshape(item_count, lat_len, values.shape[-1])
        return lax.dynamic_slice_in_dim(shaped, row_rank * lat_share, lat_share, 1).reshape(
            item_count * lat_share, values.shape[-1]
        )

    lat_flat = latents.astype(fl_type).reshape(all_rows, model_width)
    norm_a = (standard(lat_flat) * gain_rows[0]).astype(bf_type)
    queries = product(norm_a, w_mats[0]).astype(bf_type).reshape(item_count, lat_len, model_width)
    hat_pix, pull_pix = jax.vjp(standard, pixels.astype(fl_type))
    norm_p = (hat_pix * input_gain).astype(bf_type)
    key_rows = jnp.einsum("ipc,cd->ipd", norm_p, w_pairs[0], preferred_element_type=fl_type).astype(
        bf_type
    )
    value_rows = jnp.einsum(
        "ipc,cd->ipd", norm_p, w_pairs[1], preferred_element_type=fl_type
    ).astype(bf_type)
    cross_scale = model_width ** (-0.5)
    raw_scores = (
        jnp.einsum("iqd,ipd->iqp", queries, key_rows, preferred_element_type=fl_type) * cross_scale
    )
    pix_place = row_rank * pix_dev + lax.iota(jnp.int32, pix_dev)
    valid_rows = pix_place[None, :] < pix_counts[:, None]
    scores = jnp.where(valid_rows[:, None, :], raw_scores, -1e30)
    local_peak = jnp.max(scores, -1)
    peak_all = lax.pmax(local_peak, "rows")
    exp_scores = jnp.exp(scores - peak_all[:, :, None])
    total_all = lax.psum(jnp.sum(exp_scores, -1), "rows")
    attn_probs = exp_scores / total_all[:, :, None]
    probs_low = attn_probs.astype(bf_type)
    partial_out = jnp.einsum("iqp,ipd->iqd", probs_low, value_rows, preferred_element_type=fl_type)
    attended = lax.psum(partial_out, "rows")
    att_low = attended.astype(bf_type).reshape(all_rows, model_width)
    after_cross = lat_flat + product(att_low, w_mats[1])
    hat_c, pull_c = jax.vjp(standard, after_cross)
    norm_c = (hat_c * gain_rows[1]).astype(bf_type)
    gelu_c, pull_gelu_c = jax.vjp(jax.nn.gelu, product(norm_c, w_mats[2]))
    gelu_c_low = gelu_c.astype(bf_type)
    after_mlp = after_cross + product(gelu_c_low, w_mats[3])
    hat_s, pull_s = jax.vjp(standard, after_mlp)
    norm_s = (hat_s * gain_rows[2]).astype(bf_type)
    head_shape = (item_count, lat_len, HEADS, head_dim)
    q_self = product(norm_s, w_mats[4]).astype(bf_type).reshape(head_shape)
    k_self = product(norm_s, w_mats[5]).astype(bf_type).reshape(head_shape)
    v_self = product(norm_s, w_mats[6]).astype(bf_type).reshape(head_shape)
    head_scale = head_dim ** (-0.5)
    self_probs = softmax_rows(
        jnp.einsum("iqhd,ikhd->ihqk", q_self, k_self, preferred_element_type=fl_type) * head_scale
    )
    self_low = self_probs.astype(bf_type)
    mixed_heads = (
        jnp.einsum("ihqk,ikhd->iqhd", self_low, v_self, preferred_element_type=fl_type)
        .astype(bf_type)
        .reshape(all_rows, model_width)
    )
    after_self = after_mlp + product(mixed_heads, w_mats[7])
    hat_f, pull_f = jax.vjp(standard, after_self)
    norm_f = (hat_f * gain_rows[3]).astype(bf_type)
    gelu_f, pull_gelu_f = jax.vjp(jax.nn.gelu, product(norm_f, w_mats[8]))
    gelu_f_low = gelu_f.astype(bf_type)
    final_rows = after_self + product(gelu_f_low, w_mats[9])
    block_out = own_rows(final_rows).astype(bf_type).reshape(item_count, lat_share, model_width)
    mat_pairs = {}
    gain_terms = {}
    grad_out = cotangent.astype(fl_type).reshape(all_rows, model_width)
    grad_nine = grad_out.astype(bf_type)
    mat_pairs[9] = (gelu_f_low, grad_nine)
    grad_up_f = pull_gelu_f(product_nt(grad_nine, w_mats[9]))[0].astype(bf_type)
    mat_pairs[8] = (norm_f, grad_up_f)
    grad_norm_f = product_nt(grad_up_f, w_mats[8])
    gain_terms[3] = jnp.sum(own_rows(hat_f) * own_rows(grad_norm_f), 0)
    grad_self = grad_out + pull_f(grad_norm_f * gain_rows[3])[0]
    grad_seven = grad_self.astype(bf_type)
    mat_pairs[7] = (mixed_heads, grad_seven)
    grad_mixed = product_nt(grad_seven, w_mats[7]).astype(bf_type).reshape(head_shape)
    grad_self_probs = jnp.einsum(
        "iqhd,ikhd->ihqk", grad_mixed, v_self, preferred_element_type=fl_type
    )
    grad_self_scores = (
        self_probs * (grad_self_probs - jnp.sum(self_probs * grad_self_probs, -1, keepdims=True))
    ).astype(bf_type)
    grad_q_self = (
        (
            jnp.einsum("ihqk,ikhd->iqhd", grad_self_scores, k_self, preferred_element_type=fl_type)
            * head_scale
        )
        .astype(bf_type)
        .reshape(all_rows, model_width)
    )
    grad_k_self = (
        (
            jnp.einsum("ihqk,iqhd->ikhd", grad_self_scores, q_self, preferred_element_type=fl_type)
            * head_scale
        )
        .astype(bf_type)
        .reshape(all_rows, model_width)
    )
    grad_v_self = (
        jnp.einsum("ihqk,iqhd->ikhd", self_low, grad_mixed, preferred_element_type=fl_type)
        .astype(bf_type)
        .reshape(all_rows, model_width)
    )
    mat_pairs[4] = (norm_s, grad_q_self)
    mat_pairs[5] = (norm_s, grad_k_self)
    mat_pairs[6] = (norm_s, grad_v_self)
    grad_norm_s = (
        product_nt(grad_q_self, w_mats[4])
        + product_nt(grad_k_self, w_mats[5])
        + product_nt(grad_v_self, w_mats[6])
    )
    gain_terms[2] = jnp.sum(own_rows(hat_s) * own_rows(grad_norm_s), 0)
    grad_mlp = grad_self + pull_s(grad_norm_s * gain_rows[2])[0]
    grad_three = grad_mlp.astype(bf_type)
    mat_pairs[3] = (gelu_c_low, grad_three)
    grad_up_c = pull_gelu_c(product_nt(grad_three, w_mats[3]))[0].astype(bf_type)
    mat_pairs[2] = (norm_c, grad_up_c)
    grad_norm_c = product_nt(grad_up_c, w_mats[2])
    gain_terms[1] = jnp.sum(own_rows(hat_c) * own_rows(grad_norm_c), 0)
    grad_cross = grad_mlp + pull_c(grad_norm_c * gain_rows[1])[0]
    grad_one = grad_cross.astype(bf_type)
    mat_pairs[1] = (att_low, grad_one)
    grad_att = (
        product_nt(grad_one, w_mats[1]).astype(bf_type).reshape(item_count, lat_len, model_width)
    )
    grad_probs = jnp.einsum("iqd,ipd->iqp", grad_att, value_rows, preferred_element_type=fl_type)
    row_dot = lax.psum(jnp.sum(attn_probs * grad_probs, -1), "rows")
    grad_scores = (attn_probs * (grad_probs - row_dot[:, :, None])).astype(bf_type)
    query_terms = (
        jnp.einsum("iqp,ipd->iqd", grad_scores, key_rows, preferred_element_type=fl_type)
        * cross_scale
    )
    summed_query = lax.psum(query_terms, "rows")
    grad_query = lax.dynamic_slice_in_dim(summed_query, row_rank * lat_share, lat_share, 1)
    grad_query_low = grad_query.astype(bf_type).reshape(item_count * lat_share, model_width)
    first_term = product_tn(own_rows(norm_a), grad_query_low)
    grad_norm_a = product_nt(grad_query_low, w_mats[0])
    hat_own, pull_a = jax.vjp(standard, own_rows(lat_flat))
    gain_terms[0] = jnp.sum(hat_own * grad_norm_a, 0)
    latent_grad = (own_rows(grad_cross) + pull_a(grad_norm_a * gain_rows[0])[0]).reshape(
        item_count, lat_share, model_width
    )
    grad_keys = (
        jnp.einsum("iqp,iqd->ipd", grad_scores, queries, preferred_element_type=fl_type)
        * cross_scale
    ).astype(bf_type)
    grad_values = jnp.einsum(
        "iqp,iqd->ipd", probs_low, grad_att, preferred_element_type=fl_type
    ).astype(bf_type)
    key_term = jnp.einsum("ipc,ipd->cd", norm_p, grad_keys, preferred_element_type=fl_type)
    value_term = jnp.einsum("ipc,ipd->cd", norm_p, grad_values, preferred_element_type=fl_type)
    grad_norm_p = jnp.einsum(
        "ipd,cd->ipc", grad_keys, w_pairs[0], preferred_element_type=fl_type
    ) + jnp.einsum("ipd,cd->ipc", grad_values, w_pairs[1], preferred_element_type=fl_type)
    input_part = jnp.sum(hat_pix * grad_norm_p, (0, 1))
    pixel_grad = pull_pix(grad_norm_p * input_gain)[0]
    kv_terms = jnp.stack([key_term, value_term])
    gains_terms = jnp.stack([gain_terms[index] for index in range(4)])
    wide_terms = jnp.stack(
        [first_term]
        + [
            product_tn(own_rows(mat_pairs[index][0]), own_rows(mat_pairs[index][1]))
            for index in range(1, 10)
        ]
    )
    wide_grad, kv_grad, gains_grad = (
        lax.psum_scatter(wide_terms, ("dp", "rows"), scatter_dimension=1, tiled=True),
        lax.psum_scatter(kv_terms, ("dp", "rows"), scatter_dimension=2, tiled=True),
        lax.psum_scatter(gains_terms, ("dp", "rows"), scatter_dimension=1, tiled=True),
    )
    mats_first_new, mats_second_new, mats_update, mats_wsum, mats_usum = moments(
        weight_mats, wide_grad, mats_first, mats_second, (1, 2)
    )
    kv_first_new, kv_second_new, kv_update, kv_wsum, kv_usum = moments(
        kv_weights, kv_grad, kv_first, kv_second, (1, 2)
    )
    gains_first_new, gains_second_new, gains_update, gains_wsum, gains_usum = moments(
        norm_gains, gains_grad, gains_first, gains_second, (1,)
    )
    square_w = jnp.concatenate([mats_wsum, kv_wsum, gains_wsum])
    square_u = jnp.concatenate([mats_usum, kv_usum, gains_usum])
    square_w, square_u, input_grad = lax.psum((square_w, square_u, input_part), ("dp", "rows"))
    trust = jnp.sqrt(square_w) / (jnp.sqrt(square_u) + 1e-06)
    mats_new = weight_mats - step_rate * trust[0:10, None, None] * mats_update
    kv_new = kv_weights - step_rate * trust[10:12, None, None] * kv_update
    gains_new = norm_gains - step_rate * trust[12:16, None] * gains_update
    input_first_new, input_second_new, input_update, input_wsum, input_usum = moments(
        input_gain, input_grad, input_first, input_second, (0,)
    )
    input_trust = jnp.sqrt(input_wsum) / (jnp.sqrt(input_usum) + 1e-06)
    input_new = input_gain - step_rate * input_trust * input_update
    return (
        block_out,
        latent_grad,
        pixel_grad,
        wide_grad,
        kv_grad,
        gains_grad,
        input_grad,
        mats_new,
        mats_first_new,
        mats_second_new,
        kv_new,
        kv_first_new,
        kv_second_new,
        gains_new,
        gains_first_new,
        gains_second_new,
        input_new,
        input_first_new,
        input_second_new,
    )


def solution(mesh):
    in_specs = (
        P("dp", None, None),
        P("dp", "rows", None),
        P("dp"),
        P("dp", None, None),
        P(None, ("dp", "rows"), None),
        P(None, None, ("dp", "rows")),
        P(None, ("dp", "rows")),
        P(),
        P(None, ("dp", "rows"), None),
        P(None, ("dp", "rows"), None),
        P(None, None, ("dp", "rows")),
        P(None, None, ("dp", "rows")),
        P(None, ("dp", "rows")),
        P(None, ("dp", "rows")),
        P(),
        P(),
    )
    out_specs = (
        P("dp", "rows", None),
        P("dp", "rows", None),
        P("dp", "rows", None),
        P(None, ("dp", "rows"), None),
        P(None, None, ("dp", "rows")),
        P(None, ("dp", "rows")),
        P(),
        P(None, ("dp", "rows"), None),
        P(None, ("dp", "rows"), None),
        P(None, ("dp", "rows"), None),
        P(None, None, ("dp", "rows")),
        P(None, None, ("dp", "rows")),
        P(None, None, ("dp", "rows")),
        P(None, ("dp", "rows")),
        P(None, ("dp", "rows")),
        P(None, ("dp", "rows")),
        P(),
        P(),
        P(),
    )
    return jax.shard_map(local, mesh=mesh, in_specs=in_specs, out_specs=out_specs, check_vma=False)
```

profile of v0, /device:TPU:0, one launch (start us, length us, event | category | flops | bytes accessed | tf_op | source)
XLA Modules:
  0.0 1491.9 jit_solution(161498456183536272)
XLA Ops:
  12.8 43.3 %all-gather = bf16[32,32,4]{1,2,0:T(4,128)(2,1)S(1)} all-gather(bf16[1,32,4]{1,2,0:T(4,128)(2,1)S(1)} %get-tuple-element.145), channel_id=1, replica_groups=mesh['dp'=4,'rows'=8] {'dp','rows'}, dimensions={0}, use_global_device_ids=true | all-gather | bytes 8448 | tf_op jit(solution)/shard_map/all_gather | solution.py:91
  82.8 7.6 convolution_convert_fusion.1
  96.1 109.8 %all-gather.4.cloned.1.call-done = bf16[10,1024,1024]{2,1,0:T(8,128)(2,1)} async-done(((bf16[10,32,1024]{2,1,0:T(8,128)(2,1)}), bf16[10,1024,1024]{2,1,0:T(8,128)(2,1)}) %all-gather.4.cloned.1.call-update) | async-done | bytes 20971536 | tf_op jit(solution)/shard_map/all_gather | solution.py:89
  216.2 14.8 pmax.7
  234.7 14.0 psum.49
  248.7 10.8 fusion.71
  259.5 86.3 %all-reduce.7 = bf16[2,512,1024]{2,1,0:T(8,128)(2,1)} all-reduce(f32[2,512,1024]{2,1,0:T(8,128)} %fusion.71), channel_id=1, replica_groups=mesh['dp'=4,'rows'=8] {'rows'}, use_global_device_ids=true, to_apply=%region_8.9 | all-reduce | flops 1048576 | bytes 6291456 | tf_op jit(solution)/shard_map/psum | solution.py:126
  353.8 7.3 multiply_convert_fusion.8
  392.9 10.9 fusion.140
  403.8 8.0 fusion.52
  424.1 6.8 multiply_convert_fusion.5
  457.5 10.7 fusion.55
  468.2 10.5 multiply_reduce_fusion
  478.7 11.7 multiply_convert_fusion
  530.6 6.6 fusion.18
  552.1 8.4 multiply_reduce_fusion.2
  560.6 17.2 %psum.51 = f32[2,512]{1,0:T(2,128)S(1)} all-reduce(f32[2,512]{1,0:T(2,128)S(1)} %get-tuple-element.168), channel_id=1, replica_groups=mesh['dp'=4,'rows'=8] {'rows'}, use_global_device_ids=true, to_apply=%region_25.26 | all-reduce | flops 1024 | bytes 8192 | tf_op jit(solution)/shard_map/psum | solution.py:220
  577.8 6.7 multiply_convert_fusion.2
  584.5 8.6 convolution_multiply_fusion
  604.4 86.3 %all-reduce.8 = bf16[2,512,1024]{2,1,0:T(8,128)(2,1)} all-reduce(f32[2,512,1024]{2,1,0:T(8,128)} %convolution_multiply_fusion), channel_id=1, replica_groups=mesh['dp'=4,'rows'=8] {'rows'}, use_global_device_ids=true, to_apply=%region_26.27 | all-reduce | flops 1048576 | bytes 6291456 | tf_op jit(solution)/shard_map/psum | solution.py:226
  778.9 67.3 %reduce-scatter.7.cloned.1.call-done = f32[32,4]{1,0:T(8,128)} async-done(((f32[1024,4]{1,0:T(8,128)}), f32[32,4]{1,0:T(8,128)}) %reduce-scatter.7.cloned.1.call-update) | async-done | bytes 528
  847.7 138.6 %all-reduce.6.cloned.1.call-done = f32[2,261,1024]{1,0,2:T(2,128)} async-done(((f32[2,261,1024]{1,0,2:T(2,128)}), f32[2,261,1024]{1,0,2:T(2,128)}) %all-reduce.6.cloned.1.call-update) | async-done | bytes 2138128
  987.9 448.1 %reduce-scatter.5.cloned.1.call-done = f32[10,32,1024]{2,1,0:T(8,128)} async-done(((f32[10,1024,1024]{2,1,0:T(8,128)}), f32[10,32,1024]{2,1,0:T(8,128)}) %reduce-scatter.5.cloned.1.call-update) | async-done | bytes 1310736 | tf_op jit(solution)/shard_map/reduce_scatter | solution.py:260
  1440.5 36.9 %all-reduce.1 = (f32[261]{0:T(512)S(1)}, f32[16]{0:T(128)S(1)}, f32[16]{0:T(128)S(1)}) all-reduce(f32[261]{0:T(512)S(1)} %get-tuple-element.95, f32[16]{0:T(128)S(1)} %pad_maximum_fusion.3, f32[16]{0:T(128)S(1)} %pad_maximum_fusion.2), channel_id=1, replica_groups=mesh['dp'=4,'rows'=8] {'dp','rows'}, use_global_device_ids=true, to_apply=%region_41.42 | all-reduce | flops 293 | bytes 2344 | tf_op jit(solution)/shard_map/psum | solution.py:275
  (358 shorter events, 297.9 us)
Async XLA Ops:
  7.2 49.0 %copy-start.8 = (bf16[2,512,1024]{2,1,0:T(8,128)(2,1)S(1)}, bf16[2,512,1024]{2,1,0:T(8,128)(2,1)}, u32[]{:S(2)}) copy-start(bf16[2,512,1024]{2,1,0:T(8,128)(2,1)} %param.16) | copy-start | bytes 6291460
  7.2 62.3 %all-gather.6.cloned.1.call-start = ((), (), s32[]{:S(2)}) async-start(), calls=%async_computation.3 | async-start | bytes 1622016 | tf_op jit(solution)/shard_map/all_gather | solution.py:90
  9.0 196.9 %all-gather.4.cloned.1.call-start = ((), (), s32[]{:S(2)}) async-start(), calls=%async_computation.2 | async-start | bytes 21626880 | tf_op jit(solution)/shard_map/all_gather | solution.py:89
  11.3 834.8 %reduce-scatter.7.cloned.1.call-start = ((), (), s32[]{:S(2)}) async-start(), calls=%async_computation.5 | async-start | bytes 540672
  64.0 287.1 %copy-start.66 = (f32[1,1024]{1,0:T(1,128)}, f32[1,1024]{1,0:T(1,128)S(1)}, u32[]{:S(2)}) copy-start(f32[1,1024]{1,0:T(1,128)S(1)} %get-tuple-element.141) | copy-start | bytes 12292
  64.0 302.5 %copy-start.56 = (f32[1,1024]{1,0:T(1,128)}, f32[1,1024]{1,0:T(1,128)S(1)}, u32[]{:S(2)}) copy-start(f32[1,1024]{1,0:T(1,128)S(1)} %get-tuple-element.140) | copy-start | bytes 12292
  66.7 182.0 %copy-start.58 = (pred[2,1568]{1,0:T(4,128)(4,1)}, pred[2,1568]{1,0:T(4,128)(4,1)S(1)}, u32[]{:S(2)}) copy-start(pred[2,1568]{1,0:T(4,128)(4,1)S(1)} %broadcast_compare_fusion) | copy-start | bytes 9412
  231.1 28.5 %copy-start.68 = (f32[2,512]{1,0:T(2,128)}, f32[2,512]{1,0:T(2,128)S(1)}, u32[]{:S(2)}) copy-start(f32[2,512]{1,0:T(2,128)S(1)} %pmax.7) | copy-start | bytes 12292
  712.8 273.4 %all-reduce.6.cloned.1.call-start = ((), (), s32[]{:S(2)}) async-start(), calls=%async_computation.6 | async-start | bytes 6291456
  723.6 712.5 %reduce-scatter.5.cloned.1.call-start = ((), (), s32[]{:S(2)}) async-start(), calls=%async_computation.4 | async-start | bytes 43253760 | tf_op jit(solution)/shard_map/reduce_scatter | solution.py:260
  772.8 74.2 %copy-start.80 = (f32[4,32]{1,0:T(4,128)S(1)}, f32[4,32]{1,0:T(4,128)}, u32[]{:S(2)}) copy-start(f32[4,32]{1,0:T(4,128)} %param.22) | copy-start | bytes 1540
  772.8 74.2 %copy-start.88 = (f32[4,32]{1,0:T(4,128)S(1)}, f32[4,32]{1,0:T(4,128)}, u32[]{:S(2)}) copy-start(f32[4,32]{1,0:T(4,128)} %param.28) | copy-start | bytes 1540
  772.8 74.1 %copy-start.89 = (f32[4,32]{1,0:T(4,128)S(1)}, f32[4,32]{1,0:T(4,128)}, u32[]{:S(2)}) copy-start(f32[4,32]{1,0:T(4,128)} %param.29) | copy-start | bytes 1540
  772.8 214.3 %copy-start.36 = (f32[2,261,32]{1,2,0:T(8,128)S(1)}, f32[2,261,32]{1,2,0:T(8,128)}, u32[]{:S(2)}) copy-start(f32[2,261,32]{1,2,0:T(8,128)} %param.21) | copy-start | bytes 200452
  772.8 214.3 %copy-start.52 = (f32[2,261,32]{1,2,0:T(8,128)S(1)}, f32[2,261,32]{1,2,0:T(8,128)}, u32[]{:S(2)}) copy-start(f32[2,261,32]{1,2,0:T(8,128)} %param.26) | copy-start | bytes 200452
  772.8 214.3 %copy-start.53 = (f32[2,261,32]{1,2,0:T(8,128)S(1)}, f32[2,261,32]{1,2,0:T(8,128)}, u32[]{:S(2)}) copy-start(f32[2,261,32]{1,2,0:T(8,128)} %param.27) | copy-start | bytes 200452
  776.9 659.2 %copy-start.16 = (f32[10,32,1024]{2,1,0:T(8,128)S(1)}, f32[10,32,1024]{2,1,0:T(8,128)}, u32[]{:S(2)}) copy-start(f32[10,32,1024]{2,1,0:T(8,128)} %param.20) | copy-start | bytes 3932164
  846.9 593.4 %copy-start.83 = (f32[4,32]{1,0:T(4,128)}, f32[4,32]{1,0:T(4,128)S(1)}, u32[]{:S(2)}) copy-start(f32[4,32]{1,0:T(4,128)S(1)} %copy.165) | copy-start | bytes 1540
  987.2 453.2 %copy-start.87 = (f32[4]{0:T(128)S(1)}, f32[4]{0:T(128)}, u32[]{:S(2)}) copy-start(f32[4]{0:T(128)} %get-tuple-element.144) | copy-start | bytes 52
  987.2 490.3 %copy-start.84 = (f32[261]{0:T(512)S(1)}, f32[261]{0:T(512)}, u32[]{:S(2)}) copy-start(f32[261]{0:T(512)} %param.30) | copy-start | bytes 3136
  987.2 490.3 %copy-start.85 = (f32[261]{0:T(512)S(1)}, f32[261]{0:T(512)}, u32[]{:S(2)}) copy-start(f32[261]{0:T(512)} %param.31) | copy-start | bytes 3136
  987.9 496.5 %copy-start.42 = (f32[2,261,32]{1,2,0:T(8,128)}, f32[2,261,32]{1,2,0:T(8,128)S(1)}, u32[]{:S(2)}) copy-start(f32[2,261,32]{1,2,0:T(8,128)S(1)} %get-tuple-element.112) | copy-start | bytes 200452
  987.9 496.5 %copy-start.43 = (f32[2,261,32]{1,2,0:T(8,128)}, f32[2,261,32]{1,2,0:T(8,128)S(1)}, u32[]{:S(2)}) copy-start(f32[2,261,32]{1,2,0:T(8,128)S(1)} %get-tuple-element.113) | copy-start | bytes 200452
  1440.3 44.8 %copy-start.21 = (f32[10,32,1024]{2,1,0:T(8,128)}, f32[10,32,1024]{2,1,0:T(8,128)S(1)}, u32[]{:S(2)}) copy-start(f32[10,32,1024]{2,1,0:T(8,128)S(1)} %get-tuple-element.110) | copy-start | bytes 3932164
  (86 other events, 565.0 us)
Sparse Core Ops, SparseCore 0:
  11.6 57.8 all-gather.5
  73.1 132.7 all-gather.3
  713.0 133.1 reduce-scatter.6
  852.4 133.7 all-reduce.5
  988.9 447.0 reduce-scatter.4
where the time goes:
time: 1500 us; the launch traced here: 1490 us
  waiting for transfers between devices  767 us (51%)
  blocking collectives  299 us (20%)
  matrix products  264 us (18%)
  other arithmetic  75.5 us (5%)
  local copies, waits for them, and re-layouts  69.4 us (5%)
  between operations  16.9 us (1%)
    reduce_scatter x1, waiting for transfers between devices, local(): lax.psum_scatter(wide_terms, ('dp', 'rows'), scatter_dimension=1, tiled=T...  448 us
    unnamed x7, waiting for transfers between devices  206 us
    all_gather x1, waiting for transfers between devices, local(): lax.all_gather(wide_weights[0], ('dp', 'rows'), axis=1, tiled=True)  110 us
    psum x1, blocking collectives, local(): summed_query = lax.psum(query_terms, 'rows')  86.3 us
    psum x1, blocking collectives, local(): attended = lax.psum(partial_out, 'rows')  86.3 us
    dot_general x10, matrix products, product(): return jnp.dot(left_side, right_side, preferred_element_type=jnp.float32)  51.5 us
    dot_general x10, matrix products, product_nt(): lax.dot_general(left_side, right_side, (((1,), (1,)), ((), ())), preferre...  49.2 us
    all_gather x1, blocking collectives, local(): lax.all_gather(wide_weights[2], ('dp', 'rows'), axis=1, tiled=True)  43.3 us
  transfers between devices with their start and end apart: 5, of which 5 were waited for; matrix products, arithmetic and copies ran while one was open for 7% of the time, Pallas kernels for 0%

commit v1 on v0

v1 whole, which is shorter than its diff:
```python
import jax
import jax.numpy as jnp
from jax import lax
from jax.sharding import Mesh, PartitionSpec as P

HEADS = 8
first_fix = 1.0 - 0.9**10
second_fix = 1.0 - 0.999**10
step_rate = 0.25
decay_rate = 0.01
bf_type = jnp.bfloat16
fl_type = jnp.float32
ALL = ("dp", "z", "core")


def standard(values):
    centred = values - jnp.mean(values, -1, keepdims=True)
    return centred * lax.rsqrt(jnp.mean(centred * centred, -1, keepdims=True) + 1e-05)


def standard_parts(values):
    centred = values - jnp.mean(values, -1, keepdims=True)
    inv = lax.rsqrt(jnp.mean(centred * centred, -1, keepdims=True) + 1e-05)
    return centred * inv, inv


def pull(hat, inv, grad):
    return (
        grad - jnp.mean(grad, -1, keepdims=True) - hat * jnp.mean(grad * hat, -1, keepdims=True)
    ) * inv


def softmax_rows(scores):
    exp_scores = jnp.exp(scores - jnp.max(scores, -1, keepdims=True))
    return exp_scores / jnp.sum(exp_scores, -1, keepdims=True)


def product(left_side, right_side):
    return jnp.dot(left_side, right_side, preferred_element_type=fl_type)


def product_tn(left_side, right_side):
    return lax.dot_general(
        left_side, right_side, (((0,), (0,)), ((), ())), preferred_element_type=fl_type
    )


def product_nt(left_side, right_side):
    return lax.dot_general(
        left_side, right_side, (((1,), (1,)), ((), ())), preferred_element_type=fl_type
    )


def moments(weight, gradient, first_mom, second, sum_axes):
    first_new = 0.9 * first_mom + 0.1 * gradient
    second_new = 0.999 * second + 0.001 * gradient * gradient
    update = (
        first_new / first_fix / (jnp.sqrt(second_new / second_fix) + 1e-06) + decay_rate * weight
    )
    return (
        first_new,
        second_new,
        update,
        jnp.sum(weight * weight, sum_axes),
        jnp.sum(update * update, sum_axes),
    )


def swap(value):
    return lax.ppermute(value, "core", [(0, 1), (1, 0)])


def local(
    latents,
    pixels,
    pix_counts,
    cotangent,
    weight_mats,
    kv_weights,
    norm_gains,
    input_gain,
    mats_first,
    mats_second,
    kv_first,
    kv_second,
    gains_first,
    gains_second,
    input_first,
    input_second,
):
    item_count, lat_len, model_width = latents.shape
    pix_dev, pix_width = pixels.shape[1:]
    n_mats, own_width = weight_mats.shape[:2]
    n_dp, n_z = lax.axis_size("dp"), lax.axis_size("z")
    z_rank, core = lax.axis_index("z"), lax.axis_index("core")
    pad_width = -(-(pix_width + 4) // 128) * 128
    head_dim = model_width // HEADS

    kv_cols = jnp.swapaxes(kv_weights, 1, 2)
    first_block = jnp.concatenate(
        [
            weight_mats[0],
            jnp.pad(kv_cols[0], ((0, 0), (0, pad_width - pix_width))),
            kv_cols[1],
            norm_gains.T,
            jnp.zeros((own_width, pad_width - pix_width - 4), fl_type),
        ],
        axis=1,
    ).astype(bf_type)
    first_all = lax.all_gather(first_block, ALL, axis=0, tiled=True)
    w_rest = lax.all_gather(weight_mats[1:].astype(bf_type), ALL, axis=1, tiled=True)
    w_zero = first_all[:, :model_width]
    kt_zero = first_all[:, model_width : model_width + pix_width]
    kt_one = first_all[:, model_width + pad_width : model_width + pad_width + pix_width]
    gain_rows = first_all[
        :, model_width + pad_width + pix_width : model_width + pad_width + pix_width + 4
    ].T.astype(fl_type)

    def w_mat(index):
        return w_zero if index == 0 else w_rest[index - 1]

    lat_both = latents.astype(fl_type).reshape(item_count * lat_len, model_width)
    hat_both, inv_both = standard_parts(lat_both)
    norm_both = (hat_both * gain_rows[0]).astype(bf_type)
    q_both = product(norm_both, w_zero).astype(bf_type)
    cross_scale = model_width ** (-0.5)
    qk_both = (
        (product(q_both, kt_zero) * cross_scale)
        .astype(bf_type)
        .reshape(item_count, lat_len, pix_width)
    )
    hat_pix, inv_pix = standard_parts(pixels.astype(fl_type))
    norm_pix = (hat_pix * input_gain).astype(bf_type)
    scores = jnp.einsum("iqc,ipc->iqp", qk_both, norm_pix, preferred_element_type=fl_type)
    pix_place = (z_rank * 2 + core) * pix_dev + lax.iota(jnp.int32, pix_dev)
    valid_rows = pix_place[None, :] < pix_counts[:, None]
    scores = jnp.where(valid_rows[:, None, :], scores, -1e30)
    peak_loc = jnp.max(scores, -1)
    exp_scores = jnp.exp(scores - peak_loc[:, :, None])
    exp_low = exp_scores.astype(bf_type)
    total_loc = jnp.sum(exp_scores, -1)
    part_loc = jnp.einsum("iqp,ipc->iqc", exp_low, norm_pix, preferred_element_type=fl_type)
    packed = jnp.concatenate(
        [
            part_loc,
            peak_loc[:, :, None],
            total_loc[:, :, None],
            jnp.zeros((item_count, lat_len, pad_width - pix_width - 2), fl_type),
        ],
        axis=2,
    )

    def own_of(both):
        return lax.dynamic_index_in_dim(both, core, 0, keepdims=False)

    def other_of(both):
        return lax.dynamic_index_in_dim(both, 1 - core, 0, keepdims=False)

    def by_item(own, other):
        return jnp.where(core == 0, jnp.stack([own, other]), jnp.stack([other, own]))

    pair = jnp.stack([own_of(packed), swap(other_of(packed))])
    everyone = lax.all_gather(pair, "z", axis=0, tiled=True)
    peaks = everyone[:, :, pix_width]
    peak = jnp.max(peaks, 0)
    shares = jnp.exp(peaks - peak)
    total = jnp.sum(shares * everyone[:, :, pix_width + 1], 0)
    mixed_pix = jnp.sum(shares[:, :, None] * everyone[:, :, :pix_width], 0) / total[:, None]
    mixed_low = mixed_pix.astype(bf_type)

    lat_own = own_of(latents).astype(fl_type)
    hat_a = own_of(hat_both.reshape(item_count, lat_len, model_width))
    inv_a = own_of(inv_both.reshape(item_count, lat_len, 1))
    norm_a = own_of(norm_both.reshape(item_count, lat_len, model_width))
    q_own = own_of(q_both.reshape(item_count, lat_len, model_width))
    att_low = product_nt(mixed_low, kt_one).astype(bf_type)
    after_cross = lat_own + product(att_low, w_mat(1))
    hat_c, inv_c = standard_parts(after_cross)
    norm_c = (hat_c * gain_rows[1]).astype(bf_type)
    gelu_c, pull_gelu_c = jax.vjp(jax.nn.gelu, product(norm_c, w_mat(2)))
    gelu_c_low = gelu_c.astype(bf_type)
    after_mlp = after_cross + product(gelu_c_low, w_mat(3))
    hat_s, inv_s = standard_parts(after_mlp)
    norm_s = (hat_s * gain_rows[2]).astype(bf_type)
    head_shape = (lat_len, HEADS, head_dim)
    q_self = product(norm_s, w_mat(4)).astype(bf_type).reshape(head_shape)
    k_self = product(norm_s, w_mat(5)).astype(bf_type).reshape(head_shape)
    v_self = product(norm_s, w_mat(6)).astype(bf_type).reshape(head_shape)
    head_scale = head_dim ** (-0.5)
    self_probs = softmax_rows(
        jnp.einsum("qhd,khd->hqk", q_self, k_self, preferred_element_type=fl_type) * head_scale
    )
    self_low = self_probs.astype(bf_type)
    mixed_heads = (
        jnp.einsum("hqk,khd->qhd", self_low, v_self, preferred_element_type=fl_type)
        .astype(bf_type)
        .reshape(lat_len, model_width)
    )
    after_self = after_mlp + product(mixed_heads, w_mat(7))
    hat_f, inv_f = standard_parts(after_self)
    norm_f = (hat_f * gain_rows[3]).astype(bf_type)
    gelu_f, pull_gelu_f = jax.vjp(jax.nn.gelu, product(norm_f, w_mat(8)))
    gelu_f_low = gelu_f.astype(bf_type)
    z_share = lat_len // n_z

    def z_rows(values):
        return lax.dynamic_slice_in_dim(values, z_rank * z_share, z_share, 0)

    def exchange_rows(values):
        halves = values.reshape(2, z_share // 2, model_width)
        return by_item(own_of(halves), swap(other_of(halves)))

    block_out = exchange_rows(
        (z_rows(after_self) + product(z_rows(gelu_f_low), w_mat(9))).astype(bf_type)
    )

    pair_width = 2 * own_width
    n_cols = n_dp * pair_width
    wanted = lax.iota(jnp.int32, n_cols)
    wanted = ((wanted // pair_width) * n_z + z_rank) * pair_width + wanted % pair_width
    select = (lax.iota(jnp.int32, model_width)[:, None] == wanted[None, :]).astype(bf_type)

    def chosen(values):
        return product(values, select).astype(bf_type)

    def chosen_sum(values):
        total_cols = jnp.sum(values, 0).reshape(n_dp, n_z, pair_width)
        return lax.dynamic_index_in_dim(total_cols, z_rank, 1, keepdims=False).reshape(n_cols)

    grad_out = own_of(cotangent).astype(fl_type)
    grad_nine = own_of(cotangent)
    terms = {}
    gain_terms = {}
    terms[9] = product_tn(chosen(gelu_f_low), grad_nine)
    grad_up_f = pull_gelu_f(product_nt(grad_nine, w_mat(9)))[0].astype(bf_type)
    terms[8] = product_tn(chosen(norm_f), grad_up_f)
    grad_norm_f = product_nt(grad_up_f, w_mat(8))
    gain_terms[3] = chosen_sum(hat_f * grad_norm_f)
    grad_self = grad_out + pull(hat_f, inv_f, grad_norm_f * gain_rows[3])
    grad_seven = grad_self.astype(bf_type)
    terms[7] = product_tn(chosen(mixed_heads), grad_seven)
    grad_mixed = product_nt(grad_seven, w_mat(7)).astype(bf_type).reshape(head_shape)
    grad_self_probs = jnp.einsum("qhd,khd->hqk", grad_mixed, v_self, preferred_element_type=fl_type)
    grad_self_scores = (
        self_probs * (grad_self_probs - jnp.sum(self_probs * grad_self_probs, -1, keepdims=True))
    ).astype(bf_type)
    grad_q_self = (
        (
            jnp.einsum("hqk,khd->qhd", grad_self_scores, k_self, preferred_element_type=fl_type)
            * head_scale
        )
        .astype(bf_type)
        .reshape(lat_len, model_width)
    )
    grad_k_self = (
        (
            jnp.einsum("hqk,qhd->khd", grad_self_scores, q_self, preferred_element_type=fl_type)
            * head_scale
        )
        .astype(bf_type)
        .reshape(lat_len, model_width)
    )
    grad_v_self = (
        jnp.einsum("hqk,qhd->khd", self_low, grad_mixed, preferred_element_type=fl_type)
        .astype(bf_type)
        .reshape(lat_len, model_width)
    )
    norm_s_chosen = chosen(norm_s)
    terms[4] = product_tn(norm_s_chosen, grad_q_self)
    terms[5] = product_tn(norm_s_chosen, grad_k_self)
    terms[6] = product_tn(norm_s_chosen, grad_v_self)
    grad_norm_s = (
        product_nt(grad_q_self, w_mat(4))
        + product_nt(grad_k_self, w_mat(5))
        + product_nt(grad_v_self, w_mat(6))
    )
    gain_terms[2] = chosen_sum(hat_s * grad_norm_s)
    grad_mlp = grad_self + pull(hat_s, inv_s, grad_norm_s * gain_rows[2])
    grad_three = grad_mlp.astype(bf_type)
    terms[3] = product_tn(chosen(gelu_c_low), grad_three)
    grad_up_c = pull_gelu_c(product_nt(grad_three, w_mat(3)))[0].astype(bf_type)
    terms[2] = product_tn(chosen(norm_c), grad_up_c)
    grad_norm_c = product_nt(grad_up_c, w_mat(2))
    gain_terms[1] = chosen_sum(hat_c * grad_norm_c)
    grad_cross = grad_mlp + pull(hat_c, inv_c, grad_norm_c * gain_rows[1])
    grad_one = grad_cross.astype(bf_type)
    terms[1] = product_tn(chosen(att_low), grad_one)
    grad_att = product_nt(grad_one, w_mat(1)).astype(bf_type)
    gk_own = product(grad_att, kt_one).astype(bf_type)
    dot_own = jnp.sum(gk_own.astype(fl_type) * mixed_pix, -1)
    term_k_one = product_tn(chosen(grad_att), mixed_low)

    early = jnp.stack([terms[index] for index in range(1, 10)])
    early = early.reshape(9, n_dp * 2, own_width, model_width).swapaxes(0, 1)
    early = early.reshape(n_dp * 2 * 9 * own_width, model_width).astype(bf_type)
    early_sum = lax.psum_scatter(early, ("dp", "core"), scatter_dimension=0, tiled=True)
    early_grad = early_sum.astype(fl_type).reshape(9, own_width, model_width)

    stats_own = jnp.stack([peak, total, dot_own])
    stats = by_item(stats_own, swap(stats_own))
    gk_both = by_item(gk_own, swap(gk_own))
    probs = exp_low.astype(fl_type) * (jnp.exp(peak_loc - stats[:, 0]) / stats[:, 1])[:, :, None]
    grad_probs = jnp.einsum("iqc,ipc->iqp", gk_both, norm_pix, preferred_element_type=fl_type)
    grad_scores = (probs * (grad_probs - stats[:, 2][:, :, None])).astype(bf_type)
    probs_low = probs.astype(bf_type)
    query_part = jnp.einsum("iqp,ipc->iqc", grad_scores, norm_pix, preferred_element_type=fl_type)
    query_own = own_of(query_part) + swap(other_of(query_part))
    query_sum = lax.psum(query_own, "z")
    grad_norm_p = jnp.einsum(
        "iqp,iqc->ipc", grad_scores, qk_both, preferred_element_type=fl_type
    ) + jnp.einsum("iqp,iqc->ipc", probs_low, gk_both, preferred_element_type=fl_type)
    input_part = jnp.sum(hat_pix * grad_norm_p, (0, 1))
    pixel_grad = pull(hat_pix, inv_pix, grad_norm_p * input_gain)

    query_low = query_sum.astype(bf_type)
    grad_query = (product_nt(query_low, kt_zero) * cross_scale).astype(bf_type)
    term_zero = product_tn(chosen(norm_a), grad_query)
    grad_norm_a = product_nt(grad_query, w_zero)
    gain_terms[0] = chosen_sum(hat_a * grad_norm_a)
    latent_grad = exchange_rows(
        z_rows(grad_cross)
        + pull(z_rows(hat_a), z_rows(inv_a), z_rows(grad_norm_a) * gain_rows[0])
    )
    term_k_zero = product_tn(chosen(q_own), query_low) * cross_scale
    gains_cols = jnp.stack([gain_terms[index] for index in range(4)], axis=1)
    late = jnp.concatenate(
        [
            term_zero,
            jnp.pad(term_k_zero, ((0, 0), (0, pad_width - pix_width))),
            term_k_one,
            gains_cols,
            jnp.zeros((n_cols, pad_width - pix_width - 4), fl_type),
        ],
        axis=1,
    ).astype(bf_type)
    late_sum = lax.psum_scatter(late, ("dp", "core"), scatter_dimension=0, tiled=True).astype(
        fl_type
    )
    wide_grad = jnp.concatenate([late_sum[None, :, :model_width], early_grad], axis=0)
    kv_grad = jnp.stack(
        [
            late_sum[:, model_width : model_width + pix_width].T,
            late_sum[:, model_width + pad_width : model_width + pad_width + pix_width].T,
        ]
    )
    gains_grad = late_sum[
        :, model_width + pad_width + pix_width : model_width + pad_width + pix_width + 4
    ].T

    mats_first_new, mats_second_new, mats_update, mats_wsum, mats_usum = moments(
        weight_mats, wide_grad, mats_first, mats_second, (1, 2)
    )
    kv_first_new, kv_second_new, kv_update, kv_wsum, kv_usum = moments(
        kv_weights, kv_grad, kv_first, kv_second, (1, 2)
    )
    gains_first_new, gains_second_new, gains_update, gains_wsum, gains_usum = moments(
        norm_gains, gains_grad, gains_first, gains_second, (1,)
    )
    small = jnp.concatenate(
        [mats_wsum, kv_wsum, gains_wsum, mats_usum, kv_usum, gains_usum, input_part]
    )
    small = lax.psum(small, ALL)
    square_w, square_u, input_grad = small[:16], small[16:32], small[32:]
    trust = jnp.sqrt(square_w) / (jnp.sqrt(square_u) + 1e-06)
    mats_new = weight_mats - step_rate * trust[0:10, None, None] * mats_update
    kv_new = kv_weights - step_rate * trust[10:12, None, None] * kv_update
    gains_new = norm_gains - step_rate * trust[12:16, None] * gains_update
    input_first_new, input_second_new, input_update, input_wsum, input_usum = moments(
        input_gain, input_grad, input_first, input_second, (0,)
    )
    input_trust = jnp.sqrt(input_wsum) / (jnp.sqrt(input_usum) + 1e-06)
    input_new = input_gain - step_rate * input_trust * input_update
    return (
        block_out,
        latent_grad,
        pixel_grad,
        wide_grad,
        kv_grad,
        gains_grad,
        input_grad,
        mats_new,
        mats_first_new,
        mats_second_new,
        kv_new,
        kv_first_new,
        kv_second_new,
        gains_new,
        gains_first_new,
        gains_second_new,
        input_new,
        input_first_new,
        input_second_new,
    )


def solution(mesh):
    n_dp, n_rows = mesh.devices.shape
    split_mesh = Mesh(mesh.devices.reshape(n_dp, n_rows // 2, 2), ALL)
    rows = ("z", "core")
    items = P("dp", None, None)
    pix = P("dp", rows, None)
    mats = P(None, ALL, None)
    pairs = P(None, None, ALL)
    gains = P(None, ALL)
    in_specs = (
        items,
        pix,
        P("dp"),
        items,
        mats,
        pairs,
        gains,
        P(),
        mats,
        mats,
        pairs,
        pairs,
        gains,
        gains,
        P(),
        P(),
    )
    out_specs = (
        pix,
        pix,
        pix,
        mats,
        pairs,
        gains,
        P(),
        mats,
        mats,
        mats,
        pairs,
        pairs,
        pairs,
        gains,
        gains,
        gains,
        P(),
        P(),
        P(),
    )
    return jax.shard_map(
        local, mesh=split_mesh, in_specs=in_specs, out_specs=out_specs, check_vma=False
    )
```

time: 1500 us -> 680 us (0.45)
  waiting for transfers between devices: 767 us -> 336 us
  blocking collectives: 299 us -> 68 us
  matrix products: 264 us -> 148 us
  other arithmetic: 75.5 us -> 47.9 us
  local copies, waits for them, and re-layouts: 69.4 us -> 50.6 us
    reduce_scatter x1, waiting for transfers between devices: 448 us -> 51.1 us  [local(): lax.psum_scatter(early, ('dp', 'core'), scatter_dimension=0, tiled=True)]
    unnamed x7 -> x6, waiting for transfers between devices: 206 us -> 0.08 us
    psum x5 -> x2, blocking collectives: 241 us -> 68 us  [the longest x1 39.3 us: local(): small = lax.psum(small, ALL)]
    all_gather x2 -> x3, waiting for transfers between devices: 113 us -> 281 us  [the longest x1 111 us: local(): everyone = lax.all_gather(pair, 'z', axis=0, tiled=True)]
    dot_general x27 -> x25, matrix products: 165 us -> 66.7 us  [the longest x14 39.9 us: product(): return jnp.dot(left_side, right_side, preferred_element_type=fl_type)]
    all_gather x1 -> x0, blocking collectives: 43.3 us -> none  [local(): lax.all_gather(wide_weights[2], ('dp', 'rows'), axis=1, tiled=True)]
    convert_element_type x10 -> x4, other arithmetic: 23.1 us -> 3.25 us  [the longest x1 1.42 us: local(): exp_low = exp_scores.astype(bf_type)]
    dot_general x10 -> x12, matrix products: 39 us -> 31.6 us  [product_tn(): lax.dot_general(left_side, right_side, (((0,), (0,)), ((), ())), preferre...]
  transfers between devices with their start and end apart: 5 -> 11, of which waited for: 5 -> 6; matrix products, arithmetic and copies ran while one was open for 7% -> 11% of each run, Pallas kernels for 0% -> 0%
where the time goes in v1:
time: 680 us; the launch traced here: 670 us
  waiting for transfers between devices  336 us (49%)
  matrix products  148 us (22%)
  blocking collectives  68 us (10%)
  local copies, waits for them, and re-layouts  50.6 us (7%)
  other arithmetic  47.9 us (7%)
  between operations  17 us (2%)
    all_gather x1, waiting for transfers between devices, local(): everyone = lax.all_gather(pair, 'z', axis=0, tiled=True)  111 us
    all_gather x1, waiting for transfers between devices, local(): lax.all_gather(weight_mats[1:].astype(bf_type), ALL, axis=1, tiled=True)  110 us
    all_gather x1, waiting for transfers between devices, local(): first_all = lax.all_gather(first_block, ALL, axis=0, tiled=True)  60.5 us
    reduce_scatter x1, waiting for transfers between devices, local(): lax.psum_scatter(early, ('dp', 'core'), scatter_dimension=0, tiled=True)  51.1 us
    dot_general x12, matrix products, product_nt(): lax.dot_general(left_side, right_side, (((1,), (1,)), ((), ())), preferre...  42.8 us
    dot_general x14, matrix products, product(): return jnp.dot(left_side, right_side, preferred_element_type=fl_type)  39.9 us
    psum x1, blocking collectives, local(): small = lax.psum(small, ALL)  39.3 us
    dot_general x12, matrix products, product_tn(): lax.dot_general(left_side, right_side, (((0,), (0,)), ((), ())), preferre...  31.6 us
  transfers between devices with their start and end apart: 11, of which 6 were waited for; matrix products, arithmetic and copies ran while one was open for 11% of the time, Pallas kernels for 0%

profile of v1, /device:TPU:0, one launch (start us, length us, event | category | flops | bytes accessed | tf_op | source)
XLA Modules:
  0.0 669.6 jit_solution(7148499049082436399)
XLA Ops:
  14.3 60.5 %all-gather.4.cloned.1.call-done = bf16[1024,1792]{1,0:T(8,128)(2,1)} async-done(((bf16[32,1792]{1,0:T(8,128)(2,1)}), bf16[1024,1792]{1,0:T(8,128)(2,1)}) %all-gather.4.cloned.1.call-update) | async-done | bytes 3670032 | tf_op jit(solution)/shard_map/all_gather | solution.py:110
  86.3 3.9 select_reduce_fusion
  104.0 110.7 %all-gather.6.cloned.1.call-done = f32[8,512,384]{2,1,0:T(8,128)} async-done(((f32[2,512,384]{2,1,0:T(8,128)}), f32[8,512,384]{2,1,0:T(8,128)}) %all-gather.6.cloned.1.call-update) | async-done | bytes 6291472 | tf_op jit(solution)/shard_map/all_gather | solution.py:163
  214.7 5.4 fusion.205
  231.3 109.6 %all-gather.8.cloned.1.call-done = bf16[9,1024,1024]{2,1,0:T(8,128)(2,1)} async-done(((bf16[9,32,1024]{2,1,0:T(8,128)(2,1)}), bf16[9,1024,1024]{2,1,0:T(8,128)(2,1)}) %all-gather.8.cloned.1.call-update) | async-done | bytes 18874384 | tf_op jit(solution)/shard_map/all_gather | solution.py:111
  347.5 3.9 fusion.207
  358.4 4.5 fusion.76
  365.6 7.3 %fusion.208 = (f32[8,512]{1,0:T(8,128)S(1)}, f32[8,512,512]{1,2,0:T(8,128)}) fusion(bf16[512,8,128]{0,2,1:T(8,128)(2,1)} %bitcast.312, bf16[512,8,128]{0,2,1:T(8,128)(2,1)S(1)} %bitcast.310), kind=kOutput, calls=%fused_computation.368 | convolution fusion | flops 543162880 | bytes 10502144 | tf_op jit(solution)/shard_map/sub | solution.py:34
  382.0 4.7 multiply_convert_fusion.6
  386.7 4.0 fusion.39
  396.7 4.1 fusion.74
  402.3 5.4 multiply_reduce_fusion
  421.8 3.9 multiply_reduce_fusion.5
  428.2 4.8 convolution_convert_fusion.8
  432.9 5.5 fusion.32
  438.5 4.6 convolution_convert_fusion.9
  447.6 4.1 convolution_convert_fusion.10
  467.2 4.6 multiply_convert_fusion.1
  476.4 28.8 %all-reduce.3 = bf16[512,261]{0,1:T(8,128)(2,1)S(1)} all-reduce(f32[512,261]{0,1:T(8,128)S(1)} %bitcast_add_fusion), channel_id=1, replica_groups=mesh['dp'=4,'z'=4,'core'=2] {'z'}, use_global_device_ids=true, to_apply=%region_25.26 | all-reduce | flops 133632 | bytes 801792 | tf_op jit(solution)/shard_map/psum | solution.py:308
  512.3 4.9 fusion.40
  530.0 5.4 copy.296
  558.7 51.1 %reduce-scatter.5.cloned.1.call-done = bf16[288,1024]{1,0:T(8,128)(2,1)} async-done(((bf16[2304,1024]{1,0:T(8,128)(2,1)}), bf16[288,1024]{1,0:T(8,128)(2,1)}) %reduce-scatter.5.cloned.1.call-update) | async-done | bytes 589840 | tf_op jit(solution)/shard_map/reduce_scatter | solution.py:296
  611.3 4.1 multiply_reduce_fusion.16
  615.5 39.3 %psum.15 = f32[293]{0:T(512)S(1)} all-reduce(f32[293]{0:T(512)S(1)} %concatenate.23), channel_id=1, replica_groups=mesh['dp'=4,'z'=4,'core'=2] {'dp','z','core'}, use_global_device_ids=true, to_apply=%region_43.44 | all-reduce | flops 293 | bytes 2344 | tf_op jit(solution)/shard_map/psum | solution.py:362
  (355 shorter events, 167.8 us)
Async XLA Ops:
  7.2 67.6 %all-gather.4.cloned.1.call-start = ((), (), s32[]{:S(2)}) async-start(), calls=%async_computation.2 | async-start | bytes 3784704 | tf_op jit(solution)/shard_map/all_gather | solution.py:110
  10.4 204.3 %all-gather.6.cloned.1.call-start = ((), (), s32[]{:S(2)}) async-start(), calls=%async_computation.3 | async-start | bytes 7864320 | tf_op jit(solution)/shard_map/all_gather | solution.py:163
  76.9 317.5 %copy-start.61 = (f32[1024]{0:T(1024)}, f32[1024]{0:T(1024)S(1)}, u32[]{:S(2)}) copy-start(f32[1024]{0:T(1024)S(1)} %get-tuple-element.168) | copy-start | bytes 12292
  93.7 2.4 collective-permute-start
  100.4 240.5 %all-gather.8.cloned.1.call-start = ((), (), s32[]{:S(2)}) async-start(), calls=%async_computation.4 | async-start | bytes 19464192 | tf_op jit(solution)/shard_map/all_gather | solution.py:111
  101.3 454.0 %reduce-scatter.7.cloned.1.call-start = ((), (), s32[]{:S(2)}) async-start(), calls=%async_computation.6 | async-start | bytes 1032192
  101.6 403.6 %copy-start.67 = (s32[256]{0:T(256)}, s32[256]{0:T(256)S(1)}, u32[]{:S(2)}) copy-start(s32[256]{0:T(256)S(1)} %fusion.184) | copy-start | bytes 3076
  231.3 112.5 %copy-start.39 = (bf16[512,1024]{1,0:T(8,128)(2,1)}, bf16[512,1024]{1,0:T(8,128)(2,1)S(1)}, u32[]{:S(2)}) copy-start(bf16[512,1024]{1,0:T(8,128)(2,1)S(1)} %convolution_convert_fusion.1) | copy-start | bytes 3145732
  358.4 7.2 %copy-start.20 = (bf16[512,1024]{0,1:T(8,128)(2,1)}, bf16[512,1024]{0,1:T(8,128)(2,1)S(1)}, u32[]{:S(2)}) copy-start(bf16[512,1024]{0,1:T(8,128)(2,1)S(1)} %copy.318) | copy-start | bytes 3145732
  381.6 12.9 %copy-start.16 = (f32[512,1024]{1,0:T(8,128)}, f32[512,1024]{1,0:T(8,128)S(1)}, u32[]{:S(2)}) copy-start(f32[512,1024]{1,0:T(8,128)S(1)} %get-tuple-element.221) | copy-start | bytes 6291460
  381.6 12.9 %copy-start.59 = (f32[512]{0:T(512)}, f32[512]{0:T(512)S(1)}, u32[]{:S(2)}) copy-start(f32[512]{0:T(512)S(1)} %broadcast_multiply_fusion.10) | copy-start | bytes 6148
  382.0 12.5 %copy-start.63 = (f32[512]{0:T(512)}, f32[512]{0:T(512)S(1)}, u32[]{:S(2)}) copy-start(f32[512]{0:T(512)S(1)} %add_rsqrt_fusion.2) | copy-start | bytes 6148
  457.4 9.7 %collective-permute-start.2 = (f32[3,512]{1,0:T(4,128)S(1)}, f32[3,512]{1,0:T(4,128)S(1)}, u32[]{:S(2)}, u32[]{:S(2)}) collective-permute-start(f32[3,512]{1,0:T(4,128)S(1)} %pad_maximum_fusion.3), channel_id=1, source_target_pairs={{0,1},{1,0},{2,3},{3,2},{4,5},{5,4},{6,7},{7,6},{8,9},{9,8},{10,11... | collective-permute-start | bytes 18440 | tf_op jit(solution)/shard_map/ppermute | solution.py:70
  464.0 3.2 collective-permute-start.3
  473.5 2.8 collective-permute-start.4
  519.8 90.1 %reduce-scatter.5.cloned.1.call-start = ((), (), s32[]{:S(2)}) async-start(), calls=%async_computation.5 | async-start | bytes 5308416 | tf_op jit(solution)/shard_map/reduce_scatter | solution.py:296
  538.4 1.6 collective-permute-start.1
  549.8 4.7 collective-permute-start.5
  556.9 54.2 %copy-start.8 = (f32[10,32,1024]{2,1,0:T(8,128)S(1)}, f32[10,32,1024]{2,1,0:T(8,128)}, u32[]{:S(2)}) copy-start(f32[10,32,1024]{2,1,0:T(8,128)} %param.20) | copy-start | bytes 3932164
  558.7 100.3 %copy-start.46 = (f32[2,261,32]{1,2,0:T(8,128)}, f32[2,261,32]{1,2,0:T(8,128)S(1)}, u32[]{:S(2)}) copy-start(f32[2,261,32]{1,2,0:T(8,128)S(1)} %get-tuple-element.184) | copy-start | bytes 200452
  558.7 100.3 %copy-start.47 = (f32[2,261,32]{1,2,0:T(8,128)}, f32[2,261,32]{1,2,0:T(8,128)S(1)}, u32[]{:S(2)}) copy-start(f32[2,261,32]{1,2,0:T(8,128)S(1)} %get-tuple-element.185) | copy-start | bytes 200452
  611.3 43.7 %copy-start.72 = (f32[261]{0:T(512)S(1)}, f32[261]{0:T(512)}, u32[]{:S(2)}) copy-start(f32[261]{0:T(512)} %param.30) | copy-start | bytes 3136
  611.3 43.7 %copy-start.73 = (f32[261]{0:T(512)S(1)}, f32[261]{0:T(512)}, u32[]{:S(2)}) copy-start(f32[261]{0:T(512)} %param.31) | copy-start | bytes 3136
  615.5 47.3 %copy-start.17 = (f32[10,32,1024]{2,1,0:T(8,128)}, f32[10,32,1024]{2,1,0:T(8,128)S(1)}, u32[]{:S(2)}) copy-start(f32[10,32,1024]{2,1,0:T(8,128)S(1)} %get-tuple-element.187) | copy-start | bytes 3932164
  (71 other events, 216.2 us)
Sparse Core Ops, SparseCore 0:
  11.5 63.2 all-gather.3
  100.5 114.1 all-gather.5
  218.4 122.4 all-gather.7
  519.9 32.7 reduce-scatter.6
  555.9 53.8 reduce-scatter.4

commit v2 on v1

--- a/solution.py
+++ b/solution.py
@@ -1,6 +1,10 @@
+import functools
+
 import jax
 import jax.numpy as jnp
 from jax import lax
+from jax.experimental import pallas as pl
+from jax.experimental.pallas import tpu as pltpu
 from jax.sharding import Mesh, PartitionSpec as P
 
 HEADS = 8
@@ -11,6 +15,416 @@
 bf_type = jnp.bfloat16
 fl_type = jnp.float32
 ALL = ("dp", "z", "core")
+
+NT = (((1,), (1,)), ((), ()))
+TN = (((0,), (0,)), ((), ()))
+NN = (((1,), (0,)), ((), ()))
+MESH = pl.DeviceIdType.MESH
+PIECES = ((0, 3), (3, 6), (6, 9))
+
+
+def dot(left_side, right_side, dims=NN):
+    return lax.dot_general(left_side, right_side, dims, preferred_element_type=fl_type)
+
+
+def round_up(value, unit):
+    return -(-value // unit) * unit
+
+
+def tile_of(rows, unit, most):
+    best = unit
+    for size in range(unit, most + 1, unit):
+        if rows % size == 0:
+            best = size
+    return best
+
+
+def meet(peers):
+    barrier = pltpu.get_barrier_semaphore()
+    for peer in peers:
+        pl.semaphore_signal(barrier, inc=1, device_id=peer, device_id_type=MESH)
+    pl.semaphore_wait(barrier, len(peers))
+
+
+class Gather:
+    def __init__(self, mine, place, sems, n_z):
+        self.mine, self.place, self.sems, self.n_z = mine, place, sems, n_z
+        self.d, self.z, self.c = (lax.axis_index(name) for name in ALL)
+        self.z_from = [lax.rem(self.z + n_z - i, n_z) for i in range(n_z)]
+        self.z_to = [lax.rem(self.z + i, n_z) for i in range(n_z)]
+        self.sent = []
+
+    def slot(self, d, z, c):
+        return self.place((d * self.n_z + z) * 2 + c)
+
+    def copy(self, src, shard, kind, index, peer):
+        return pltpu.make_async_remote_copy(
+            src_ref=src,
+            dst_ref=self.slot(*shard),
+            send_sem=self.sems.at[0, kind, index],
+            recv_sem=self.sems.at[1, kind, index],
+            device_id=peer,
+            device_id_type=MESH,
+        )
+
+    def send(self, src, shard, kind, index, peer):
+        copy = self.copy(src, shard, kind, index, peer)
+        copy.start()
+        self.sent.append(copy)
+
+    def arrived(self, shard, kind, index):
+        self.copy(self.mine, shard, kind, index, (self.d, self.z, 1 - self.c)).wait_recv()
+
+    def start(self, local_sem):
+        d, z, c = self.d, self.z, self.c
+        shard = (d, z, c)
+        for i in range(1, self.n_z):
+            self.send(self.mine, shard, 0, i, (d, self.z_to[i], c))
+        self.send(self.mine, shard, 1, 0, (d ^ 1, z, c))
+        self.send(self.mine, shard, 2, 0, (d ^ 2, z, c))
+        self.send(self.mine, shard, 4, 0, (d, z, 1 - c))
+        self.own = pltpu.make_async_copy(self.mine, self.slot(*shard), local_sem)
+        self.own.start()
+
+    def relay_z(self):
+        d, z, c = self.d, self.z, self.c
+        for i in range(1, self.n_z):
+            shard = (d, self.z_from[i], c)
+            self.arrived(shard, 0, i)
+            src = self.slot(*shard)
+            self.send(src, shard, 1, i, (d ^ 1, z, c))
+            self.send(src, shard, 2, i, (d ^ 2, z, c))
+            self.send(src, shard, 4, i, (d, z, 1 - c))
+
+    def relay_plane(self):
+        d, z, c = self.d, self.z, self.c
+        for i in range(self.n_z):
+            for kind, flip, onward in ((1, 1, 2), (2, 2, 1)):
+                shard = (d ^ flip, self.z_from[i], c)
+                self.arrived(shard, kind, i)
+                src = self.slot(*shard)
+                if (i < self.n_z // 2) == (kind == 1):
+                    self.send(src, shard, 3, i, (d ^ onward, z, c))
+                self.send(src, shard, 4 + kind, i, (d, z, 1 - c))
+
+    def relay_far(self):
+        d, z, c = self.d, self.z, self.c
+        for i in range(self.n_z):
+            shard = (d ^ 3, self.z_from[i], c)
+            self.arrived(shard, 3, i)
+            self.send(self.slot(*shard), shard, 7, i, (d, z, 1 - c))
+
+    def finish(self):
+        self.own.wait()
+        for i in range(self.n_z):
+            for kind, flip in ((4, 0), (5, 1), (6, 2), (7, 3)):
+                self.arrived((self.d ^ flip, self.z_from[i], 1 - self.c), kind, i)
+
+    def drain(self):
+        for copy in self.sent:
+            copy.wait_send()
+
+
+def pixels_forward(
+    n_z,
+    gathers,
+    pix_width,
+    chunk,
+    counts,
+    first_ref,
+    *refs,
+):
+    refs = list(refs)
+    rest_ref = refs.pop(0) if gathers else None
+    pix_ref, lat_ref, gain_ref = refs[:3]
+    refs = refs[3:]
+    first_out = refs.pop(0) if gathers else None
+    rest_out = refs.pop(0) if gathers else None
+    xn_ref, pt_ref, peak_ref, qk_ref, q_ref, gains_ref, mean_ref, stat_ref = refs[:8]
+    refs = refs[8:]
+    (
+        first_all,
+        q_all,
+        s_buf,
+        px_own,
+        px_tx,
+        px_rx,
+        st_tx,
+        st_rx,
+        px2_tx,
+        px2_rx,
+        st2_tx,
+        st2_rx,
+        fin_tx,
+        fin_rx,
+        col_sems,
+        local_sems,
+    ) = refs[:16]
+    gather_sems = refs[16:]
+    d, z, c = (lax.axis_index(name) for name in ALL)
+    peers = [(d, lax.rem(z + i, n_z), c) for i in range(1, n_z)] + [(d, z, 1 - c)]
+    if gathers:
+        peers += [(d ^ 1, z, c), (d ^ 2, z, c)]
+    meet(peers)
+    if gathers:
+        own = first_ref.shape[0]
+
+        def first_place(rank):
+            return first_all.at[pl.ds(pl.multiple_of(rank * own, own), own)]
+
+        def rest_place(low, high):
+            def place(rank):
+                return rest_out.at[low:high, pl.ds(pl.multiple_of(rank * own, own), own)]
+
+            return place
+
+        first = Gather(first_ref, first_place, gather_sems[0], n_z)
+        first.start(local_sems.at[0])
+        rest = [
+            Gather(
+                rest_ref.at[low:high],
+                rest_place(low, high),
+                gather_sems[1 + index],
+                n_z,
+            )
+            for index, (low, high) in enumerate(PIECES)
+        ]
+        for index, piece in enumerate(rest):
+            piece.start(local_sems.at[1 + index])
+    else:
+        rest = []
+        load = pltpu.make_async_copy(first_ref, first_all, local_sems.at[0])
+        load.start()
+
+    n_items, pix_dev, _ = pix_ref.shape
+    lat_len, width = lat_ref.shape[1:]
+    pad_width = xn_ref.shape[2]
+    rows = tile_of(pix_dev, 16, 256)
+    tiles = pix_dev // rows
+    held = chunk * n_z
+
+    def normalise(item):
+        def body(t, _):
+            at = pl.ds(pl.multiple_of(t * rows, rows), rows)
+            values = pix_ref[item, at, :].astype(fl_type)
+            centred = values - jnp.sum(values, -1, keepdims=True) * (1.0 / pix_width)
+            var = jnp.sum(centred * centred, -1, keepdims=True) * (1.0 / pix_width)
+            normal = centred * lax.rsqrt(var + 1e-05) * gain_ref[...]
+            xn_ref[item, at, pad_width - 128 :] = jnp.zeros((rows, 128), bf_type)
+            xn_ref[item, at, :pix_width] = normal.astype(bf_type)
+            return 0
+
+        lax.fori_loop(0, tiles, body, 0)
+
+    normalise(0)
+    if gathers:
+        first.relay_z()
+    for item in range(1, n_items):
+        normalise(item)
+    if gathers:
+        first.relay_plane()
+        rest[0].relay_z()
+        first.relay_far()
+        first.finish()
+    else:
+        load.wait()
+
+    gain_at = round_up(pix_width, 8) - (pad_width - 128)
+    tail = first_all[:, width + 2 * pad_width - 128 :].astype(fl_type).T
+    gains_ref[...] = tail[gain_at : gain_at + 8]
+    lat_rows = tile_of(lat_len, 16, 256)
+    for item in range(n_items):
+
+        def queries(t, _, item=item):
+            at = pl.ds(pl.multiple_of(t * lat_rows, lat_rows), lat_rows)
+            values = lat_ref[item, at, :].astype(fl_type)
+            centred = values - jnp.mean(values, -1, keepdims=True)
+            var = jnp.mean(centred * centred, -1, keepdims=True)
+            normal = (centred * lax.rsqrt(var + 1e-05) * gains_ref[:1]).astype(bf_type)
+            q_low = dot(normal, first_all[:, :width]).astype(bf_type)
+            q_all[item, at, :] = q_low
+            raw = dot(q_low, first_all[:, width : width + pad_width])
+            qk_ref[item, at, :] = (raw * width**-0.5).astype(bf_type)
+            return 0
+
+        lax.fori_loop(0, lat_len // lat_rows, queries, 0)
+    if gathers:
+        rest[0].relay_plane()
+        rest[1].relay_z()
+
+    base = (z * 2 + c) * pix_dev
+    for item in range(n_items):
+        valid = counts[item] - base
+
+        def score(t, most, item=item, valid=valid):
+            at = pl.ds(pl.multiple_of(t * rows, rows), rows)
+            values = dot(xn_ref[item, at, :], qk_ref[item], NT)
+            place = lax.broadcasted_iota(jnp.int32, values.shape, 0) + t * rows
+            values = jnp.where(place < valid, values, -1e30)
+            s_buf[at, :] = values
+            return jnp.maximum(most, jnp.max(values.reshape(rows // 8, 8, lat_len), 0))
+
+        most = lax.fori_loop(0, tiles, score, jnp.full((8, lat_len), -1e30, fl_type))
+        peak = jnp.max(most, 0, keepdims=True)
+
+        def weigh(t, total, item=item, peak=peak):
+            at = pl.ds(pl.multiple_of(t * rows, rows), rows)
+            values = jnp.exp(s_buf[at, :] - peak)
+            pt_ref[item, at, :] = values.astype(bf_type)
+            return total + jnp.sum(values.reshape(rows // 8, 8, lat_len), 0)
+
+        total = lax.fori_loop(0, tiles, weigh, jnp.zeros((8, lat_len), fl_type))
+        total = jnp.sum(total, 0, keepdims=True)
+        peak_ref[item] = jnp.broadcast_to(peak, (8, lat_len))
+        st_tx[item, :8] = jnp.broadcast_to(peak, (8, lat_len))
+        st_tx[item, 8:] = jnp.broadcast_to(total, (8, lat_len))
+        part = dot(xn_ref[item], pt_ref[item], TN)
+        px_own[item, : part.shape[0]] = part
+        if held > part.shape[0]:
+            px_own[item, part.shape[0] :] = jnp.zeros((px_own.shape[1] - part.shape[0], lat_len), fl_type)
+        px_tx[item] = px_own[item, :held].astype(bf_type)
+
+    def column_copy(src, dst, index, peer):
+        return pltpu.make_async_remote_copy(
+            src_ref=src,
+            dst_ref=dst,
+            send_sem=col_sems.at[0, index],
+            recv_sem=col_sems.at[1, index],
+            device_id=peer,
+            device_id_type=MESH,
+        )
+
+    pair = [
+        column_copy(px_tx.at[1 - c], px_rx, 0, (d, z, 1 - c)),
+        column_copy(st_tx.at[1 - c], st_rx, 1, (d, z, 1 - c)),
+    ]
+    for copy in pair:
+        copy.start()
+    if gathers:
+        rest[0].relay_far()
+    q_ref[...] = q_all[c]
+    for copy in pair:
+        copy.wait()
+    peak_own, peak_rx = st_tx[c, :1], st_rx[:1]
+    peak = jnp.maximum(peak_own, peak_rx)
+    scale_own, scale_rx = jnp.exp(peak_own - peak), jnp.exp(peak_rx - peak)
+    st2_tx[:8] = jnp.broadcast_to(peak, (8, lat_len))
+    st2_tx[8:] = jnp.broadcast_to(scale_own * st_tx[c, 8:9] + scale_rx * st_rx[8:9], (8, lat_len))
+    both = px_own[c, :held] * scale_own + px_rx[...].astype(fl_type) * scale_rx
+    px2_tx[...] = both.astype(bf_type).reshape(n_z, chunk, lat_len)
+    copies = []
+    for i in range(1, n_z):
+        to = lax.rem(z + i, n_z)
+        copies.append(column_copy(px2_tx.at[to], px2_rx.at[z], 2 * i, (d, to, c)))
+        copies.append(column_copy(st2_tx, st2_rx.at[z], 2 * i + 1, (d, to, c)))
+    for copy in copies:
+        copy.start()
+    for copy in copies:
+        copy.wait()
+    peak = st2_tx[:1]
+    froms = [lax.rem(z + n_z - i, n_z) for i in range(1, n_z)]
+    for other in froms:
+        peak = jnp.maximum(peak, st2_rx[other, :1])
+    scale = jnp.exp(st2_tx[:1] - peak)
+    total = scale * st2_tx[8:9]
+    mean = scale * px2_tx[z].astype(fl_type)
+    for other in froms:
+        scale = jnp.exp(st2_rx[other, :1] - peak)
+        total = total + scale * st2_rx[other, 8:9]
+        mean = mean + scale * px2_rx[other].astype(fl_type)
+    stat_ref[:8] = jnp.broadcast_to(peak, (8, lat_len))
+    stat_ref[8:] = jnp.broadcast_to(total, (8, lat_len))
+    fin_tx[...] = (mean / total).astype(bf_type)
+    copies = []
+    for i in range(1, n_z):
+        to = lax.rem(z + i, n_z)
+        copies.append(column_copy(fin_tx, fin_rx.at[z], 2 * n_z + i, (d, to, c)))
+    for copy in copies:
+        copy.start()
+    if gathers:
+        rest[1].relay_plane()
+        rest[2].relay_z()
+    for copy in copies:
+        copy.wait()
+    for other in froms:
+        mean_ref[pl.ds(other * chunk, chunk)] = fin_rx[other]
+    mean_ref[pl.ds(z * chunk, chunk)] = fin_tx[...]
+    if gathers:
+        out = pltpu.make_async_copy(first_all, first_out, local_sems.at[4])
+        out.start()
+        rest[1].relay_far()
+        rest[2].relay_plane()
+        rest[2].relay_far()
+        for piece in rest:
+            piece.finish()
+        for piece in [first] + rest:
+            piece.drain()
+        out.wait()
+
+
+def forward_call(first_block, rest_block, pixels, latents, counts, input_gain, n_z, n_dev):
+    gathers = rest_block is not None
+    own, block_width = first_block.shape
+    n_items, pix_dev, pix_width = pixels.shape
+    lat_len, width = latents.shape[1:]
+    pad_width = (block_width - width) // 2
+    whole_rows = own * n_dev if gathers else own
+    chunk = round_up(-(-pix_width // n_z), 16)
+    held = chunk * n_z
+    vmem, hbm = pl.BlockSpec(memory_space=pltpu.VMEM), pl.BlockSpec(memory_space=pl.ANY)
+    shape = jax.ShapeDtypeStruct
+    in_specs = [pl.BlockSpec(memory_space=pltpu.SMEM), hbm] + [hbm] * gathers + [vmem] * 3
+    out_shape = [
+        shape((n_items, pix_dev, pad_width), bf_type),
+        shape((n_items, pix_dev, lat_len), bf_type),
+        shape((n_items, 8, lat_len), fl_type),
+        shape((n_items, lat_len, pad_width), bf_type),
+        shape((lat_len, width), bf_type),
+        shape((8, width), fl_type),
+        shape((held, lat_len), bf_type),
+        shape((16, lat_len), fl_type),
+    ]
+    out_specs = [vmem] * len(out_shape)
+    if gathers:
+        out_shape = [
+            shape((whole_rows, block_width), bf_type),
+            shape((rest_block.shape[0], whole_rows, width), bf_type),
+        ] + out_shape
+        out_specs = [hbm, hbm] + out_specs
+    scratch = [
+        pltpu.VMEM((whole_rows, block_width), bf_type),
+        pltpu.VMEM((n_items, lat_len, width), bf_type),
+        pltpu.VMEM((pix_dev, lat_len), fl_type),
+        pltpu.VMEM((n_items, max(held, pad_width), lat_len), fl_type),
+        pltpu.VMEM((n_items, held, lat_len), bf_type),
+        pltpu.VMEM((held, lat_len), bf_type),
+        pltpu.VMEM((n_items, 16, lat_len), fl_type),
+        pltpu.VMEM((16, lat_len), fl_type),
+        pltpu.VMEM((n_z, chunk, lat_len), bf_type),
+        pltpu.VMEM((n_z, chunk, lat_len), bf_type),
+        pltpu.VMEM((16, lat_len), fl_type),
+        pltpu.VMEM((n_z, 16, lat_len), fl_type),
+        pltpu.VMEM((chunk, lat_len), bf_type),
+        pltpu.VMEM((n_z, chunk, lat_len), bf_type),
+        pltpu.SemaphoreType.DMA((2, 3 * n_z)),
+        pltpu.SemaphoreType.DMA((5,)),
+    ]
+    if gathers:
+        scratch += [pltpu.SemaphoreType.DMA((2, 8, n_z))] * (1 + len(PIECES))
+    args = [counts, first_block] + ([rest_block] if gathers else [])
+    args += [pixels, latents, input_gain.reshape(1, pix_width)]
+    outs = pl.pallas_call(
+        functools.partial(pixels_forward, n_z, gathers, pix_width, chunk),
+        out_shape=out_shape,
+        in_specs=in_specs,
+        out_specs=out_specs,
+        scratch_shapes=scratch,
+        compiler_params=pltpu.CompilerParams(
+            collective_id=0, has_side_effects=True, vmem_limit_bytes=60 * 2**20
+        ),
+        name="pixels_forward",
+    )(*args)
+    return outs if gathers else [first_block, None] + list(outs)
 
 
 def standard(values):
@@ -93,63 +507,47 @@
     n_mats, own_width = weight_mats.shape[:2]
     n_dp, n_z = lax.axis_size("dp"), lax.axis_size("z")
     z_rank, core = lax.axis_index("z"), lax.axis_index("core")
-    pad_width = -(-(pix_width + 4) // 128) * 128
+    pad_width = round_up(round_up(pix_width, 8) + 8, 128)
     head_dim = model_width // HEADS
 
     kv_cols = jnp.swapaxes(kv_weights, 1, 2)
+    gain_at = round_up(pix_width, 8)
     first_block = jnp.concatenate(
         [
             weight_mats[0],
             jnp.pad(kv_cols[0], ((0, 0), (0, pad_width - pix_width))),
-            kv_cols[1],
+            jnp.pad(kv_cols[1], ((0, 0), (0, gain_at - pix_width))),
             norm_gains.T,
-            jnp.zeros((own_width, pad_width - pix_width - 4), fl_type),
+            jnp.zeros((own_width, pad_width - gain_at - 4), fl_type),
         ],
         axis=1,
     ).astype(bf_type)
-    first_all = lax.all_gather(first_block, ALL, axis=0, tiled=True)
-    w_rest = lax.all_gather(weight_mats[1:].astype(bf_type), ALL, axis=1, tiled=True)
+    rest_block = weight_mats[1:].astype(bf_type)
+    if own_width % 16:
+        first_block = lax.all_gather(first_block, ALL, axis=0, tiled=True)
+        w_rest = lax.all_gather(rest_block, ALL, axis=1, tiled=True)
+        rest_block = None
+    outs = forward_call(
+        first_block, rest_block, pixels, latents, pix_counts, input_gain, n_z, n_dp * n_z * 2
+    )
+    first_all, gathered = outs[:2]
+    xn, exp_low, peak_loc, qk_both, q_own, gain_rows, mean_rows, stat_rows = outs[2:]
+    if gathered is not None:
+        w_rest = gathered
     w_zero = first_all[:, :model_width]
     kt_zero = first_all[:, model_width : model_width + pix_width]
     kt_one = first_all[:, model_width + pad_width : model_width + pad_width + pix_width]
-    gain_rows = first_all[
-        :, model_width + pad_width + pix_width : model_width + pad_width + pix_width + 4
-    ].T.astype(fl_type)
+    norm_pix = xn[:, :, :pix_width]
+    qk_both = qk_both[:, :, :pix_width]
+    peak_loc = peak_loc[:, 0]
+    mixed_low = mean_rows[:pix_width].T
+    mixed_pix = mixed_low.astype(fl_type)
+    peak, total = stat_rows[0], stat_rows[8]
+    cross_scale = model_width ** (-0.5)
 
     def w_mat(index):
         return w_zero if index == 0 else w_rest[index - 1]
 
-    lat_both = latents.astype(fl_type).reshape(item_count * lat_len, model_width)
-    hat_both, inv_both = standard_parts(lat_both)
-    norm_both = (hat_both * gain_rows[0]).astype(bf_type)
-    q_both = product(norm_both, w_zero).astype(bf_type)
-    cross_scale = model_width ** (-0.5)
-    qk_both = (
-        (product(q_both, kt_zero) * cross_scale)
-        .astype(bf_type)
-        .reshape(item_count, lat_len, pix_width)
-    )
-    hat_pix, inv_pix = standard_parts(pixels.astype(fl_type))
-    norm_pix = (hat_pix * input_gain).astype(bf_type)
-    scores = jnp.einsum("iqc,ipc->iqp", qk_both, norm_pix, preferred_element_type=fl_type)
-    pix_place = (z_rank * 2 + core) * pix_dev + lax.iota(jnp.int32, pix_dev)
-    valid_rows = pix_place[None, :] < pix_counts[:, None]
-    scores = jnp.where(valid_rows[:, None, :], scores, -1e30)
-    peak_loc = jnp.max(scores, -1)
-    exp_scores = jnp.exp(scores - peak_loc[:, :, None])
-    exp_low = exp_scores.astype(bf_type)
-    total_loc = jnp.sum(exp_scores, -1)
-    part_loc = jnp.einsum("iqp,ipc->iqc", exp_low, norm_pix, preferred_element_type=fl_type)
-    packed = jnp.concatenate(
-        [
-            part_loc,
-            peak_loc[:, :, None],
-            total_loc[:, :, None],
-            jnp.zeros((item_count, lat_len, pad_width - pix_width - 2), fl_type),
-        ],
-        axis=2,
-    )
-
     def own_of(both):
         return lax.dynamic_index_in_dim(both, core, 0, keepdims=False)
 
@@ -159,20 +557,9 @@
     def by_item(own, other):
         return jnp.where(core == 0, jnp.stack([own, other]), jnp.stack([other, own]))
 
-    pair = jnp.stack([own_of(packed), swap(other_of(packed))])
-    everyone = lax.all_gather(pair, "z", axis=0, tiled=True)
-    peaks = everyone[:, :, pix_width]
-    peak = jnp.max(peaks, 0)
-    shares = jnp.exp(peaks - peak)
-    total = jnp.sum(shares * everyone[:, :, pix_width + 1], 0)
-    mixed_pix = jnp.sum(shares[:, :, None] * everyone[:, :, :pix_width], 0) / total[:, None]
-    mixed_low = mixed_pix.astype(bf_type)
-
     lat_own = own_of(latents).astype(fl_type)
-    hat_a = own_of(hat_both.reshape(item_count, lat_len, model_width))
-    inv_a = own_of(inv_both.reshape(item_count, lat_len, 1))
-    norm_a = own_of(norm_both.reshape(item_count, lat_len, model_width))
-    q_own = own_of(q_both.reshape(item_count, lat_len, model_width))
+    hat_a, inv_a = standard_parts(lat_own)
+    norm_a = (hat_a * gain_rows[0]).astype(bf_type)
     att_low = product_nt(mixed_low, kt_one).astype(bf_type)
     after_cross = lat_own + product(att_low, w_mat(1))
     hat_c, inv_c = standard_parts(after_cross)
@@ -296,19 +683,20 @@
     early_sum = lax.psum_scatter(early, ("dp", "core"), scatter_dimension=0, tiled=True)
     early_grad = early_sum.astype(fl_type).reshape(9, own_width, model_width)
 
+    hat_pix, inv_pix = standard_parts(pixels.astype(fl_type))
     stats_own = jnp.stack([peak, total, dot_own])
     stats = by_item(stats_own, swap(stats_own))
     gk_both = by_item(gk_own, swap(gk_own))
-    probs = exp_low.astype(fl_type) * (jnp.exp(peak_loc - stats[:, 0]) / stats[:, 1])[:, :, None]
-    grad_probs = jnp.einsum("iqc,ipc->iqp", gk_both, norm_pix, preferred_element_type=fl_type)
-    grad_scores = (probs * (grad_probs - stats[:, 2][:, :, None])).astype(bf_type)
+    probs = exp_low.astype(fl_type) * (jnp.exp(peak_loc - stats[:, 0]) / stats[:, 1])[:, None, :]
+    grad_probs = jnp.einsum("ipc,iqc->ipq", norm_pix, gk_both, preferred_element_type=fl_type)
+    grad_scores = (probs * (grad_probs - stats[:, 2][:, None, :])).astype(bf_type)
     probs_low = probs.astype(bf_type)
-    query_part = jnp.einsum("iqp,ipc->iqc", grad_scores, norm_pix, preferred_element_type=fl_type)
+    query_part = jnp.einsum("ipq,ipc->iqc", grad_scores, norm_pix, preferred_element_type=fl_type)
     query_own = own_of(query_part) + swap(other_of(query_part))
     query_sum = lax.psum(query_own, "z")
     grad_norm_p = jnp.einsum(
-        "iqp,iqc->ipc", grad_scores, qk_both, preferred_element_type=fl_type
-    ) + jnp.einsum("iqp,iqc->ipc", probs_low, gk_both, preferred_element_type=fl_type)
+        "ipq,iqc->ipc", grad_scores, qk_both, preferred_element_type=fl_type
+    ) + jnp.einsum("ipq,iqc->ipc", probs_low, gk_both, preferred_element_type=fl_type)
     input_part = jnp.sum(hat_pix * grad_norm_p, (0, 1))
     pixel_grad = pull(hat_pix, inv_pix, grad_norm_p * input_gain)
 

time: 680 us -> 497 us (0.73)
  waiting for transfers between devices: 336 us -> 54.2 us
  Pallas kernels: 0 us -> 118 us
  other arithmetic: 47.9 us -> 31.2 us
  blocking collectives: 68 us -> 76.8 us
    all_gather x3 -> x0, waiting for transfers between devices: 281 us -> none  [the longest x1 111 us: local(): everyone = lax.all_gather(pair, 'z', axis=0, tiled=True)]
    pallas_call x0 -> x1, Pallas kernels: none -> 118 us  [forward_call(): pl.pallas_call(functools.partial(pixels_forward, n_z, gathers, pix_width,...]
    psum x1, blocking collectives: 28.8 us -> 37.4 us  [local(): query_sum = lax.psum(query_own, 'z')]
    dot_general x6 -> x4, matrix products: 16.8 us -> 11.2 us  [the longest x1 5.09 us: local(): jnp.einsum('ipc,iqc->ipq', norm_pix, gk_both, preferred_element_type=fl_t...]
    unnamed x180 -> x159, local copies, waits for them, and re-layouts: 23.7 us -> 19.4 us
    dot_general x14 -> x12, matrix products: 39.9 us -> 37.7 us  [product(): return jnp.dot(left_side, right_side, preferred_element_type=fl_type)]
  transfers between devices with their start and end apart: 11 -> 7, of which waited for: 6 -> 2; matrix products, arithmetic and copies ran while one was open for 11% -> 14% of each run, Pallas kernels for 0% -> 0%
where the time goes in v2:
time: 497 us; the launch traced here: 491 us
  matrix products  147 us (30%)
  Pallas kernels  118 us (24%)
  blocking collectives  76.8 us (15%)
  waiting for transfers between devices  54.2 us (11%)
  local copies, waits for them, and re-layouts  45.7 us (9%)
  other arithmetic  31.2 us (6%)
  between operations  17 us (3%)
    pallas_call x1, Pallas kernels, forward_call(): pl.pallas_call(functools.partial(pixels_forward, n_z, gathers, pix_width,...  118 us
    reduce_scatter x1, waiting for transfers between devices, local(): lax.psum_scatter(early, ('dp', 'core'), scatter_dimension=0, tiled=True)  53.7 us
    dot_general x12, matrix products, product_nt(): lax.dot_general(left_side, right_side, (((1,), (1,)), ((), ())), preferre...  43.3 us
    psum x1, blocking collectives, local(): small = lax.psum(small, ALL)  39.3 us
    dot_general x12, matrix products, product(): return jnp.dot(left_side, right_side, preferred_element_type=fl_type)  37.7 us
    psum x1, blocking collectives, local(): query_sum = lax.psum(query_own, 'z')  37.4 us
    dot_general x12, matrix products, product_tn(): lax.dot_general(left_side, right_side, (((0,), (0,)), ((), ())), preferre...  30.6 us
    unnamed x159, local copies, waits for them, and re-layouts  19.4 us
  transfers between devices with their start and end apart: 7, of which 2 were waited for; matrix products, arithmetic and copies ran while one was open for 14% of the time, Pallas kernels for 0%

profile of v2, /device:TPU:0, one launch (start us, length us, event | category | flops | bytes accessed | tf_op | source)
XLA Modules:
  0.0 490.8 jit_solution(7455514730690110777)
XLA Ops:
  11.1 4.3 copy.144.refs_1_
  16.1 117.7 %pixels_forward.1 = (bf16[1024,1792]{1,0:T(8,128)(2,1)}, bf16[9,1024,1024]{2,1,0:T(8,128)(2,1)}, bf16[2,1568,384]{2,1,0:T(8,128)(2,1)}, bf16[2,1568,512]{2,1,0:T...) custom-call(s32[2]{0:T(128)} %counts.1, ...), custom_call_target="tpu_custom_call" | custom-call | tf_op jit(solution)/shard_map/pixels_forward/pallas_call | solution.py:416
  143.9 3.9 fusion.242
  148.5 4.2 fusion.135
  152.7 3.8 fusion.123
  156.5 3.8 fusion.120
  165.0 7.4 %fusion.243 = (f32[8,512]{1,0:T(8,128)S(1)}, f32[8,512,512]{1,2,0:T(8,128)}) fusion(bf16[512,8,128]{0,2,1:T(8,128)(2,1)S(1)} %bitcast.275, bf16[512,8,128]{0,2,1:T(8,128)(2,1)} %bitcast.277), kind=kOutput, calls=%fused_computation.351 | convolution fusion | flops 543162880 | bytes 10502144 | tf_op jit(solution)/shard_map/sub | solution.py:448
  172.4 4.6 fusion.108
  180.8 4.7 multiply_convert_fusion.6
  185.5 4.0 fusion.39
  199.6 5.3 %fusion.111 = bf16[8,128,512]{2,1,0:T(8,128)(2,1)S(1)} fusion(bf16[512,8,128]{0,2,1:T(8,128)(2,1)} %bitcast.285, f32[8,512,512]{1,2,0:T(8,128)} %get-tuple-element.177, f32[8,512]{1,0:T(8,128)S(1)} %get-tuple-element.176), kind=kOutput, calls=%fused_computation.147 | convolution fusion | flops 541589504 | bytes 10502144 | tf_op jit(solution)/shard_map/hqk,qhd->khd/dot_general | solution.py:651
  205.0 4.3 multiply_reduce_fusion
  226.7 4.7 fusion.32
  231.5 4.2 multiply_reduce_fusion.5
  236.5 4.0 fusion.114
  247.6 4.6 convolution_convert_fusion.7
  252.2 4.1 convolution_convert_fusion.8
  277.8 5.1 %multiply_convert_fusion.1 = bf16[2,1568,512]{2,1,0:T(8,128)(2,1)S(1)} fusion(bf16[2,1568,512]{2,1,0:T(8,128)(2,1)} %get-tuple-element.33, f32[2,512]{1,0:T(2,128)S(1)} %bitcast.314, f32[2,512]{1,0:T(2,128)S(1)} %bitcast.312, bf16[2,1568,384]{2,1,0:T(8,128)(2,1)} %get-tuple-element.36, bf16[1,512,261]{1,2,0:T(8,128)(2,1)} %bitcast.35, ...), kind=kOutput, calls=%fused_computation.6 | convolution fusion | flops 846969856 | bytes 9373697 | tf_op jit(solution)/shard_map/ipc,iqc->ipq/dot_general | solution.py:691
  287.9 37.4 %all-reduce.4 = bf16[512,261]{0,1:T(8,128)(2,1)S(1)} all-reduce(f32[512,261]{0,1:T(8,128)S(1)} %bitcast_add_fusion), channel_id=1, replica_groups=mesh['dp'=4,'z'=4,'core'=2] {'z'}, use_global_device_ids=true, to_apply=%region_16.17 | all-reduce | flops 133632 | bytes 801792 | tf_op jit(solution)/shard_map/psum | solution.py:696
  330.4 5.2 %multiply_reduce_fusion.6 = (bf16[1024]{0:T(1024)(128)(2,1)S(1)}, f32[512,1024]{1,0:T(8,128)}, f32[512,1024]{1,0:T(8,128)}) fusion(f32[512]{0:T(512)S(1)} %copy-done.61, f32[512]{0:T(512)S(1)} %copy-done.51, bf16[2,512,1024]{2,1,0:T(8,128)(2,1)S(1)} %copy-done.9, s32[]{:T(128)S(6)} %select_n.83, bf16[512,1024]{1,0:T(8,128)(2,1)} %multiply_convert_fusion.3, ...), kind=kOutput, calls=%fused_computation.93 | convolution fusion | flops 1076362240 | bytes 8394756 | tf_op jit(solution)/shard_map/dot_general | solution.py:463
  351.0 5.4 %copy.171 = bf16[8,9,32,1024]{3,2,1,0:T(8,128)(2,1)} copy(bf16[8,9,32,1024]{3,2,0,1:T(8,128)(2,1)} %bitcast.62) | data formatting | bytes 9437184 | tf_op jit(solution)/shard_map/convert_element_type | solution.py:682
  377.3 53.7 %reduce-scatter.5.cloned.1.call-done = bf16[288,1024]{1,0:T(8,128)(2,1)} async-done(((bf16[2304,1024]{1,0:T(8,128)(2,1)}), bf16[288,1024]{1,0:T(8,128)(2,1)}) %reduce-scatter.5.cloned.1.call-update) | async-done | bytes 589840 | tf_op jit(solution)/shard_map/reduce_scatter | solution.py:683
  432.5 3.9 multiply_reduce_fusion.16
  436.5 39.3 %psum.15 = f32[293]{0:T(512)S(1)} all-reduce(f32[293]{0:T(512)S(1)} %concatenate.19), channel_id=1, replica_groups=mesh['dp'=4,'z'=4,'core'=2] {'dp','z','core'}, use_global_device_ids=true, to_apply=%region_38.39 | all-reduce | flops 293 | bytes 2344 | tf_op jit(solution)/shard_map/psum | solution.py:750
  (300 shorter events, 134.1 us)
Async XLA Ops:
  7.2 366.5 %reduce-scatter.7.cloned.1.call-start = ((), (), s32[]{:S(2)}) async-start(), calls=%async_computation.3 | async-start | bytes 1032192
  134.8 58.4 %copy-start.48 = (f32[1,1024]{1,0:T(1,128)}, f32[1,1024]{1,0:T(1,128)S(1)}, u32[]{:S(2)}) copy-start(f32[1,1024]{1,0:T(1,128)S(1)} %get-tuple-element.160) | copy-start | bytes 12292
  148.5 8.1 %copy-start.26 = (bf16[512,1024]{1,0:T(8,128)(2,1)}, bf16[512,1024]{1,0:T(8,128)(2,1)S(1)}, u32[]{:S(2)}) copy-start(bf16[512,1024]{1,0:T(8,128)(2,1)S(1)} %multiply_convert_fusion.8) | copy-start | bytes 3145732
  161.9 10.5 %copy-start.18 = (bf16[512,1024]{0,1:T(8,128)(2,1)}, bf16[512,1024]{0,1:T(8,128)(2,1)S(1)}, u32[]{:S(2)}) copy-start(bf16[512,1024]{0,1:T(8,128)(2,1)S(1)} %copy.194) | copy-start | bytes 3145732
  180.4 12.9 %copy-start.12 = (f32[512,1024]{1,0:T(8,128)}, f32[512,1024]{1,0:T(8,128)S(1)}, u32[]{:S(2)}) copy-start(f32[512,1024]{1,0:T(8,128)S(1)} %get-tuple-element.179) | copy-start | bytes 6291460
  180.4 12.9 %copy-start.46 = (f32[512]{0:T(512)}, f32[512]{0:T(512)S(1)}, u32[]{:S(2)}) copy-start(f32[512]{0:T(512)S(1)} %broadcast_multiply_fusion.10) | copy-start | bytes 6148
  180.8 12.5 %copy-start.52 = (f32[512]{0:T(512)}, f32[512]{0:T(512)S(1)}, u32[]{:S(2)}) copy-start(f32[512]{0:T(512)S(1)} %add_rsqrt_fusion.2) | copy-start | bytes 6148
  199.6 9.7 %slice-start = ((s8[8388608]{0:T(1024)(128)(4,1)}), s8[4194304]{0:T(1024)(128)(4,1)S(1)}, s32[]{:S(2)}) async-start(s8[8388608]{0:T(1024)(128)(4,1)} %bitcast.267), calls=%async_computation.4 | async-start | bytes 8388608
  226.7 9.0 %copy-start.7 = (f32[512,1024]{1,0:T(8,128)}, f32[512,1024]{1,0:T(8,128)S(1)}, u32[]{:S(2)}) copy-start(f32[512,1024]{1,0:T(8,128)S(1)} %multiply_add_fusion.1) | copy-start | bytes 6291460
  236.4 19.9 %copy-start.6 = (f32[512,1024]{1,0:T(8,128)}, f32[512,1024]{1,0:T(8,128)S(1)}, u32[]{:S(2)}) copy-start(f32[512,1024]{1,0:T(8,128)S(1)} %multiply_add_fusion) | copy-start | bytes 6291460
  243.9 32.3 %collective-permute-start.1 = (f32[3,512]{1,0:T(4,128)}, f32[3,512]{1,0:T(4,128)}, u32[]{:S(2)}, u32[]{:S(2)}) collective-permute-start(f32[3,512]{1,0:T(4,128)} %get-tuple-element.168), channel_id=1, source_target_pairs={{0,1},{1,0},{2,3},{3,2},{4,5},{5,4},{6,7},{7,6},{8,9},{9,8},{10,11... | collective-permute-start | bytes 18440 | tf_op jit(solution)/shard_map/ppermute | solution.py:484
  244.5 33.3 %collective-permute-start.2 = (bf16[512,261]{0,1:T(8,128)(2,1)}, bf16[512,261]{0,1:T(8,128)(2,1)}, u32[]{:S(2)}, u32[]{:S(2)}) collective-permute-start(bf16[512,261]{0,1:T(8,128)(2,1)} %get-tuple-element.188), channel_id=1, source_target_pairs={{0,1},{1,0},{2,3},{3,2},{4,5},{5,4},{6,7},{7,6},{8,9},{9,8},{10,11... | collective-permute-start | bytes 801800 | tf_op jit(solution)/shard_map/ppermute | solution.py:484
  245.9 13.7 %copy-start.54 = (s32[256]{0:T(256)}, s32[256]{0:T(256)S(1)}, u32[]{:S(2)}) copy-start(s32[256]{0:T(256)S(1)} %fusion.225) | copy-start | bytes 3076
  284.6 3.2 collective-permute-start.3
  287.9 40.3 %copy-start.55 = (s32[256]{0:T(256)S(1)}, s32[256]{0:T(256)}, u32[]{:S(2)}) copy-start(s32[256]{0:T(256)} %copy-done.54) | copy-start | bytes 3076
  340.8 90.2 %reduce-scatter.5.cloned.1.call-start = ((), (), s32[]{:S(2)}) async-start(), calls=%async_computation.2 | async-start | bytes 5308416 | tf_op jit(solution)/shard_map/reduce_scatter | solution.py:683
  358.9 1.4 collective-permute-start
  368.2 4.7 collective-permute-start.4
  375.1 57.2 %copy-start.5 = (f32[10,32,1024]{2,1,0:T(8,128)S(1)}, f32[10,32,1024]{2,1,0:T(8,128)}, u32[]{:S(2)}) copy-start(f32[10,32,1024]{2,1,0:T(8,128)} %param.20) | copy-start | bytes 3932164
  377.3 102.7 %copy-start.38 = (f32[2,261,32]{1,2,0:T(8,128)}, f32[2,261,32]{1,2,0:T(8,128)S(1)}, u32[]{:S(2)}) copy-start(f32[2,261,32]{1,2,0:T(8,128)S(1)} %get-tuple-element.143) | copy-start | bytes 200452
  377.3 102.7 %copy-start.39 = (f32[2,261,32]{1,2,0:T(8,128)}, f32[2,261,32]{1,2,0:T(8,128)S(1)}, u32[]{:S(2)}) copy-start(f32[2,261,32]{1,2,0:T(8,128)S(1)} %get-tuple-element.144) | copy-start | bytes 200452
  432.5 43.5 %copy-start.59 = (f32[261]{0:T(512)S(1)}, f32[261]{0:T(512)}, u32[]{:S(2)}) copy-start(f32[261]{0:T(512)} %param.30) | copy-start | bytes 3136
  432.5 43.5 %copy-start.60 = (f32[261]{0:T(512)S(1)}, f32[261]{0:T(512)}, u32[]{:S(2)}) copy-start(f32[261]{0:T(512)} %param.31) | copy-start | bytes 3136
  436.4 47.4 %copy-start.13 = (f32[10,32,1024]{2,1,0:T(8,128)}, f32[10,32,1024]{2,1,0:T(8,128)S(1)}, u32[]{:S(2)}) copy-start(f32[10,32,1024]{2,1,0:T(8,128)S(1)} %get-tuple-element.146) | copy-start | bytes 3932164
  (57 other events, 172.1 us)
Sparse Core Ops, SparseCore 0:
  340.9 32.6 reduce-scatter.6
  377.1 53.8 reduce-scatter.4

commit v3 on v2

--- a/solution.py
+++ b/solution.py
@@ -427,6 +427,475 @@
     return outs if gathers else [first_block, None] + list(outs)
 
 
+def remote(src, dst, sems, index, peer):
+    return pltpu.make_async_remote_copy(
+        src_ref=src,
+        dst_ref=dst,
+        send_sem=sems.at[0, index],
+        recv_sem=sems.at[1, index],
+        device_id=peer,
+        device_id_type=MESH,
+    )
+
+
+def backward(n_z, n_dp, pix_width, chunk, *refs):
+    (
+        gk_ref,
+        stats_ref,
+        early_ref,
+        block_ref,
+        xn_hbm,
+        pt_hbm,
+        peak_ref,
+        qk_ref,
+        pix_hbm,
+        gain_ref,
+        lat_hbm,
+        first_hbm,
+        gains_ref,
+        q_hbm,
+        cross_ref,
+        k_one_ref,
+        gterm_ref,
+        mats_hbm,
+        mfirst_hbm,
+        msecond_hbm,
+        kv_ref,
+        kfirst_ref,
+        ksecond_ref,
+        ng_ref,
+        gfirst_ref,
+        gsecond_ref,
+        block_out,
+        lat_out,
+        pix_out,
+        mats_out,
+        kv_out,
+        gains_out,
+        small_out,
+        xn,
+        pt,
+        pix,
+        lat,
+        first,
+        q_own,
+        mats,
+        mfirst,
+        msecond,
+        gk_rx,
+        stats_rx,
+        ds,
+        pl_low,
+        part_tx,
+        part_own,
+        part_rx,
+        col_tx,
+        col_rx,
+        fin_tx,
+        fin_rx,
+        dst_full,
+        early_own,
+        early_rx,
+        early_tx,
+        early_sum,
+        early_far,
+        pix_buf,
+        hat,
+        inv,
+        norm,
+        dq,
+        da,
+        sel,
+        lat_tx,
+        late,
+        late_rx,
+        late_tx,
+        late_own,
+        late_far,
+        small_tx,
+        small_col,
+        small_far_tx,
+        small_far,
+        input_acc,
+        sems,
+        loads,
+    ) = refs
+    d, z, c = (lax.axis_index(name) for name in ALL)
+    oc = 1 - c
+    n_items, pix_dev, pad_width = xn.shape
+    lat_len, width = lat.shape[1:]
+    own = kv_out.shape[2]
+    far = [lax.rem(d + i, n_dp) for i in range(1, n_dp)]
+    far_from = [lax.rem(d + n_dp - i, n_dp) for i in range(1, n_dp)]
+    z_to = [lax.rem(z + i, n_z) for i in range(1, n_z)]
+    z_from = [lax.rem(z + n_z - i, n_z) for i in range(1, n_z)]
+    partner = (d, z, oc)
+    column = [(i, 0) for i in range(1, n_z)] + [(i, 1) for i in range(n_z)]
+
+    def in_column(i, j):
+        return (d, lax.rem(z + i, n_z), lax.rem(c + j, 2))
+
+    meet([in_column(i, j) for i, j in column] + [(to, z, c) for to in far])
+
+    slot = iter(range(1000))
+
+    def send(src, dst, peer):
+        copy = remote(src, dst, sems, next(slot), peer)
+        copy.start()
+        return copy
+
+    pair = [
+        send(gk_ref, gk_rx, partner),
+        send(stats_ref, stats_rx, partner),
+    ]
+    out_pair = send(block_ref.at[oc], block_out.at[c], partner)
+    early_pair = send(early_ref.at[:, oc], early_rx, partner)
+    load_slot = iter(range(1000))
+
+    def load(src, dst):
+        copy = pltpu.make_async_copy(src, dst, loads.at[next(load_slot)])
+        copy.start()
+        return copy
+
+    l_xn = load(xn_hbm, xn)
+    l_pt = load(pt_hbm, pt)
+    l_pix = load(pix_hbm, pix)
+    l_lat = load(lat_hbm.at[c], lat.at[0])
+    l_first = load(first_hbm, first)
+    l_q = load(q_hbm, q_own)
+    l_early = load(early_ref.at[:, c], early_own)
+    l_mats = [load(mats_hbm, mats), load(mfirst_hbm, mfirst), load(msecond_hbm, msecond)]
+    block_out[c] = block_ref[c]
+
+    rows = tile_of(pix_dev, 16, 256)
+    tiles = pix_dev // rows
+    held = chunk * n_z
+    l_pt.wait()
+    l_xn.wait()
+    for copy in pair:
+        copy.wait()
+
+    def score_side(item, gk, stats):
+        scale = jnp.exp(peak_ref[item, :1] - stats[0, :1]) / stats[1, :1]
+        delta = stats[2, :1]
+
+        def body(t, _):
+            at = pl.ds(pl.multiple_of(t * rows, rows), rows)
+            probs = pt[item, at, :].astype(fl_type) * scale
+            grad_probs = dot(xn[item, at, :], gk[...], NT)
+            ds[item, at, :] = (probs * (grad_probs - delta)).astype(bf_type)
+            pl_low[item, at, :] = probs.astype(bf_type)
+            return 0
+
+        lax.fori_loop(0, tiles, body, 0)
+        return dot(xn[item], ds[item], TN)
+
+    part_tx[...] = score_side(oc, gk_rx, stats_rx)[: part_tx.shape[0]].astype(part_tx.dtype)
+    px_pair = send(part_tx, part_rx, partner)
+    part_own[...] = score_side(c, gk_ref, stats_ref)
+    l_early.wait()
+    early_pair.wait()
+
+    n_rows = early_own.shape[1]
+
+    def pair_sum(t, _):
+        both = early_own[t].astype(fl_type) + early_rx[t].astype(fl_type)
+        early_tx[t] = both.astype(early_tx.dtype)
+        return 0
+
+    lax.fori_loop(0, n_dp, pair_sum, 0)
+    early_sum[...] = early_own[d].astype(fl_type) + early_rx[d].astype(fl_type)
+    px_pair.wait()
+    both = part_own[: part_rx.shape[0]] + part_rx[...].astype(fl_type)
+    if held > both.shape[0]:
+        both = jnp.concatenate([both, jnp.zeros((held - both.shape[0], lat_len), fl_type)], 0)
+    col_tx[...] = both[:held].astype(col_tx.dtype).reshape(n_z, chunk, lat_len)
+    col = [
+        send(col_tx.at[to], col_rx.at[z], (d, to, c)) for to in z_to
+    ]
+    early_out = [send(early_tx.at[to], early_far.at[d], (to, z, c)) for to in far]
+
+    l_pix.wait()
+    input_acc[...] = jnp.zeros(input_acc.shape, fl_type)
+
+    def pixel_side(item, gk):
+        def body(t, _):
+            at = pl.ds(pl.multiple_of(t * rows, rows), rows)
+            grad = dot(ds[item, at, :], qk_ref[item]) + dot(pl_low[item, at, :], gk[...])
+            grad = grad[:, :pix_width]
+            values = pix[item, at, :].astype(fl_type)
+            centred = values - jnp.sum(values, -1, keepdims=True) * (1.0 / pix_width)
+            var = jnp.sum(centred * centred, -1, keepdims=True) * (1.0 / pix_width)
+            scale = lax.rsqrt(var + 1e-05)
+            normal = centred * scale
+            input_acc[...] += jnp.sum((normal * grad).reshape(rows // 8, 8, pix_width), 0)
+            grad = grad * gain_ref[...]
+            mean = jnp.sum(grad, -1, keepdims=True) * (1.0 / pix_width)
+            along = jnp.sum(grad * normal, -1, keepdims=True) * (1.0 / pix_width)
+            pix_buf[item, at, :] = (grad - mean - normal * along) * scale
+            return 0
+
+        lax.fori_loop(0, tiles, body, 0)
+        return load(pix_buf.at[item], pix_out.at[item])
+
+    stores = [pixel_side(c, gk_ref)]
+
+    for copy in col:
+        copy.wait()
+    mean = col_tx[z].astype(fl_type)
+    for other in z_from:
+        mean = mean + col_rx[other].astype(fl_type)
+    fin_tx[...] = mean.astype(fin_tx.dtype)
+    fin = [send(fin_tx, fin_rx.at[z], (d, to, c)) for to in z_to]
+
+    stores.append(pixel_side(oc, gk_rx))
+
+    l_lat.wait()
+    l_first.wait()
+    l_q.wait()
+    pair_width = 2 * own
+    n_cols = n_dp * pair_width
+    wanted = lax.broadcasted_iota(jnp.int32, (width, n_cols), 1)
+    wanted = (lax.div(wanted, pair_width) * n_z + z) * pair_width + lax.rem(wanted, pair_width)
+    place = lax.broadcasted_iota(jnp.int32, (width, n_cols), 0)
+    sel[...] = jnp.where(place == wanted, 1.0, 0.0).astype(bf_type)
+    values = lat[0].astype(fl_type)
+    centred = values - jnp.mean(values, -1, keepdims=True)
+    scale = lax.rsqrt(jnp.mean(centred * centred, -1, keepdims=True) + 1e-05)
+    hat[...] = centred * scale
+    inv[...] = jnp.broadcast_to(scale, inv.shape)
+    norm[...] = dot((hat[...] * gains_ref[:1]).astype(bf_type), sel[...]).astype(bf_type)
+
+    for copy in fin:
+        copy.wait()
+    dst_full[...] = jnp.zeros(dst_full.shape, fl_type)
+    for other in z_from:
+        dst_full[pl.ds(other * chunk, chunk)] = fin_rx[other].astype(fl_type)
+    dst_full[pl.ds(z * chunk, chunk)] = fin_tx[...].astype(fl_type)
+    summed = dst_full[:pad_width].T.astype(bf_type)
+    kt_zero = first[:, width : width + pad_width]
+    dq[...] = (dot(summed, kt_zero, NT) * width**-0.5).astype(bf_type)
+    da[...] = dot(dq[...], first[:, :width], NT)
+    term_zero = dot(norm[...], dq[...], TN)
+    q_sel = dot(q_own[...], sel[...]).astype(bf_type)
+    term_k = dot(q_sel, summed, TN) * width**-0.5
+    gain_at = round_up(pix_width, 8) - (pad_width - 128)
+    gain_zero = jnp.sum(hat[...] * da[...], 0, keepdims=True)
+    place = lax.broadcasted_iota(jnp.int32, (8, width), 0)
+    gain_sums = jnp.where(place == 0, gain_zero, gterm_ref[...]).astype(bf_type)
+    gain_cols = dot(gain_sums, sel[...])
+    gain_cols = jnp.concatenate(
+        [
+            jnp.zeros((gain_at, n_cols), fl_type),
+            gain_cols,
+            jnp.zeros((128 - gain_at - 8, n_cols), fl_type),
+        ],
+        0,
+    ).T
+    late_shape = (n_dp, 2, own, -1)
+    late[:, :, :, :width] = term_zero.astype(late.dtype).reshape(n_dp, 2, own, width)
+    late[:, :, :, width : width + pad_width] = term_k.astype(late.dtype).reshape(
+        n_dp, 2, own, pad_width
+    )
+    ones = k_one_ref[...]
+    late[:, :, :, width + pad_width : width + 2 * pad_width - 128] = (
+        ones[:, : pad_width - 128].astype(late.dtype).reshape(n_dp, 2, own, pad_width - 128)
+    )
+    late[:, :, :, width + 2 * pad_width - 128 :] = (
+        (ones[:, pad_width - 128 :] + gain_cols).astype(late.dtype).reshape(n_dp, 2, own, 128)
+    )
+    late_pair = send(late.at[:, oc], late_rx, partner)
+
+    z_share = lat_len // n_z
+    at = pl.ds(pl.multiple_of(z * z_share, z_share), z_share)
+    grad = da[at, :] * gains_ref[:1]
+    normal = hat[at, :]
+    mean = jnp.mean(grad, -1, keepdims=True)
+    along = jnp.mean(grad * normal, -1, keepdims=True)
+    lat_grad = cross_ref[...] + (grad - mean - normal * along) * inv[at, :1]
+    lat_tx[...] = lat_grad.reshape(2, z_share // 2, width)
+    lat_pair = send(lat_tx.at[oc], lat_out.at[c], partner)
+    lat_out[c] = lat_tx[c]
+
+    late_pair.wait()
+    late_sum = late[:, c].astype(fl_type) + late_rx[...].astype(fl_type)
+    late_tx[...] = late_sum.astype(late_tx.dtype)
+    late_out = [send(late_tx.at[to], late_far.at[d], (to, z, c)) for to in far]
+    late_own[...] = late[d, c].astype(fl_type) + late_rx[d].astype(fl_type)
+
+    for copy in early_out:
+        copy.wait()
+    for copy in l_mats:
+        copy.wait()
+    lane = lax.broadcasted_iota(jnp.int32, (1, 128), 1)
+
+    def norms(weight, gradient, first_mom, second):
+        first_new = 0.9 * first_mom + 0.1 * gradient
+        second_new = 0.999 * second + 0.001 * gradient * gradient
+        update = (
+            first_new / first_fix / (jnp.sqrt(second_new / second_fix) + 1e-06)
+            + decay_rate * weight
+        )
+        return (weight * weight, update * update)
+
+    def total(values):
+        return jnp.sum(jnp.sum(values, 0, keepdims=True), 1, keepdims=True)
+
+    def matrix(k, sums):
+        at = pl.ds(pl.multiple_of((k - 1) * own, own), own)
+        gradient = early_sum[at, :]
+        for other in far_from:
+            gradient = gradient + early_far[other, at, :].astype(fl_type)
+        mats_out[k] = gradient
+        w_sq, u_sq = norms(mats[k], gradient, mfirst[k], msecond[k])
+        here = lane == k
+        return (
+            sums[0] + jnp.where(here, total(w_sq), 0.0),
+            sums[1] + jnp.where(here, total(u_sq), 0.0),
+        )
+
+    zero = jnp.zeros((1, 128), fl_type)
+    sums = lax.fori_loop(1, mats.shape[0], matrix, (zero, zero))
+
+    for copy in late_out:
+        copy.wait()
+    for other in far_from:
+        late_own[...] += late_far[other].astype(fl_type)
+    mats_out[0] = late_own[:, :width]
+    grads = [(mats[0], late_own[:, :width], mfirst[0], msecond[0], 0)]
+    for k in range(2):
+        cols = late_own[:, width + k * pad_width : width + (k + 1) * pad_width].T
+        kv_out[k] = cols[:pix_width]
+        grads.append((kv_ref[k], cols[:pix_width], kfirst_ref[k], ksecond_ref[k], 10 + k))
+    at = pad_width - 128 + gain_at
+    gain_grad = cols[at : at + 8]
+    gains_out[...] = gain_grad[:4]
+    w_sum, u_sum = sums
+    for weight, gradient, first_mom, second, k in grads:
+        w_sq, u_sq = norms(weight, gradient, first_mom, second)
+        w_sum = w_sum + jnp.where(lane == k, total(w_sq), 0.0)
+        u_sum = u_sum + jnp.where(lane == k, total(u_sq), 0.0)
+    w_sq, u_sq = norms(ng_ref[...], gain_grad[:4], gfirst_ref[...], gsecond_ref[...])
+    w_sq, u_sq = jnp.sum(w_sq, 1, keepdims=True), jnp.sum(u_sq, 1, keepdims=True)
+    for k in range(4):
+        w_sum = w_sum + jnp.where(lane == 12 + k, w_sq[k : k + 1], 0.0)
+        u_sum = u_sum + jnp.where(lane == 12 + k, u_sq[k : k + 1], 0.0)
+    small_tx[...] = jnp.zeros(small_tx.shape, fl_type)
+    small_tx[0:1, :128] = w_sum
+    small_tx[1:2, :128] = u_sum
+    small_tx[2:3, :pix_width] = jnp.sum(input_acc[...], 0, keepdims=True)
+    copies = [
+        send(small_tx, small_col.at[n], in_column(i, j)) for n, (i, j) in enumerate(column)
+    ]
+    for copy in copies:
+        copy.wait()
+    all_sum = small_tx[...]
+    for n in range(len(column)):
+        all_sum = all_sum + small_col[n]
+    small_far_tx[...] = all_sum
+    copies = [
+        send(small_far_tx, small_far.at[n], (to, z, c)) for n, to in enumerate(far)
+    ]
+    for copy in copies:
+        copy.wait()
+    for n in range(len(far)):
+        all_sum = all_sum + small_far[n]
+    small_out[...] = all_sum
+    for copy in [out_pair, lat_pair] + stores:
+        copy.wait()
+
+
+def backward_call(n_z, n_dp, args):
+    (gk, stats, early, block, xn, pt, _, qk, pixels, _, latents, first) = args[:12]
+    mats, kv, gains = args[17], args[20], args[23]
+    n_items, pix_dev, pix_width = pixels.shape
+    lat_len, width = latents.shape[1:]
+    pad_width = xn.shape[2]
+    own = mats.shape[1]
+    early_rows = early.shape[2]
+    wire = early.dtype
+    chunk = round_up(-(-pix_width // n_z), 16)
+    held = chunk * n_z
+    cut = min(held, pad_width)
+    z_share = lat_len // n_z
+    n_cols = n_dp * 2 * own
+    vmem, hbm = pl.BlockSpec(memory_space=pltpu.VMEM), pl.BlockSpec(memory_space=pl.ANY)
+    in_hbm = {"early": 2, "xn": 4, "pt": 5, "pix": 8, "lat": 10, "first": 11, "q": 13}
+    places = set(in_hbm.values()) | {17, 18, 19}
+    in_specs = [hbm if index in places else vmem for index in range(len(args))]
+    shape, buf = jax.ShapeDtypeStruct, pltpu.VMEM
+    out_shape = [
+        shape((n_items, z_share // 2, width), bf_type),
+        shape((n_items, z_share // 2, width), fl_type),
+        shape(pixels.shape, fl_type),
+        shape(mats.shape, fl_type),
+        shape(kv.shape, fl_type),
+        shape(gains.shape, fl_type),
+        shape((8, pad_width), fl_type),
+    ]
+    out_specs = [vmem, vmem, hbm, vmem, vmem, vmem, vmem]
+    late_width = width + 2 * pad_width
+    scratch = [
+        buf(xn.shape, bf_type),
+        buf(pt.shape, bf_type),
+        buf(pixels.shape, bf_type),
+        buf((1, lat_len, width), bf_type),
+        buf(first.shape, bf_type),
+        buf((lat_len, width), bf_type),
+        buf(mats.shape, fl_type),
+        buf(mats.shape, fl_type),
+        buf(mats.shape, fl_type),
+        buf(gk.shape, bf_type),
+        buf(stats.shape, fl_type),
+        buf(pt.shape, bf_type),
+        buf(pt.shape, bf_type),
+        buf((cut, lat_len), bf_type),
+        buf((pad_width, lat_len), fl_type),
+        buf((cut, lat_len), bf_type),
+        buf((n_z, chunk, lat_len), bf_type),
+        buf((n_z, chunk, lat_len), bf_type),
+        buf((chunk, lat_len), bf_type),
+        buf((n_z, chunk, lat_len), bf_type),
+        buf((max(held, pad_width), lat_len), fl_type),
+        buf((n_dp, early_rows, width), wire),
+        buf((n_dp, early_rows, width), wire),
+        buf((n_dp, early_rows, width), wire),
+        buf((early_rows, width), fl_type),
+        buf((n_dp, early_rows, width), wire),
+        buf(pixels.shape, fl_type),
+        buf((lat_len, width), fl_type),
+        buf((lat_len, 128), fl_type),
+        buf((lat_len, n_cols), bf_type),
+        buf((lat_len, width), bf_type),
+        buf((lat_len, width), fl_type),
+        buf((width, n_cols), bf_type),
+        buf((2, z_share // 2, width), fl_type),
+        buf((n_dp, 2, own, late_width), wire),
+        buf((n_dp, own, late_width), wire),
+        buf((n_dp, own, late_width), wire),
+        buf((own, late_width), fl_type),
+        buf((n_dp, own, late_width), wire),
+        buf((8, pad_width), fl_type),
+        buf((2 * n_z - 1, 8, pad_width), fl_type),
+        buf((8, pad_width), fl_type),
+        buf((n_dp - 1, 8, pad_width), fl_type),
+        buf((8, pix_width), fl_type),
+        pltpu.SemaphoreType.DMA((2, 20 + 6 * n_z + 3 * n_dp)),
+        pltpu.SemaphoreType.DMA((16,)),
+    ]
+    return pl.pallas_call(
+        functools.partial(backward, n_z, n_dp, pix_width, chunk),
+        out_shape=out_shape,
+        in_specs=in_specs,
+        out_specs=out_specs,
+        scratch_shapes=scratch,
+        compiler_params=pltpu.CompilerParams(
+            collective_id=1, has_side_effects=True, vmem_limit_bytes=60 * 2**20
+        ),
+        name="backward",
+    )(*args)
+
+
 def standard(values):
     centred = values - jnp.mean(values, -1, keepdims=True)
     return centred * lax.rsqrt(jnp.mean(centred * centred, -1, keepdims=True) + 1e-05)
@@ -478,10 +947,6 @@
         jnp.sum(weight * weight, sum_axes),
         jnp.sum(update * update, sum_axes),
     )
-
-
-def swap(value):
-    return lax.ppermute(value, "core", [(0, 1), (1, 0)])
 
 
 def local(
@@ -537,13 +1002,9 @@
     w_zero = first_all[:, :model_width]
     kt_zero = first_all[:, model_width : model_width + pix_width]
     kt_one = first_all[:, model_width + pad_width : model_width + pad_width + pix_width]
-    norm_pix = xn[:, :, :pix_width]
-    qk_both = qk_both[:, :, :pix_width]
-    peak_loc = peak_loc[:, 0]
     mixed_low = mean_rows[:pix_width].T
     mixed_pix = mixed_low.astype(fl_type)
     peak, total = stat_rows[0], stat_rows[8]
-    cross_scale = model_width ** (-0.5)
 
     def w_mat(index):
         return w_zero if index == 0 else w_rest[index - 1]
@@ -553,9 +1014,6 @@
 
     def other_of(both):
         return lax.dynamic_index_in_dim(both, 1 - core, 0, keepdims=False)
-
-    def by_item(own, other):
-        return jnp.where(core == 0, jnp.stack([own, other]), jnp.stack([other, own]))
 
     lat_own = own_of(latents).astype(fl_type)
     hat_a, inv_a = standard_parts(lat_own)
@@ -593,13 +1051,8 @@
     def z_rows(values):
         return lax.dynamic_slice_in_dim(values, z_rank * z_share, z_share, 0)
 
-    def exchange_rows(values):
-        halves = values.reshape(2, z_share // 2, model_width)
-        return by_item(own_of(halves), swap(other_of(halves)))
-
-    block_out = exchange_rows(
-        (z_rows(after_self) + product(z_rows(gelu_f_low), w_mat(9))).astype(bf_type)
-    )
+    block_rows = (z_rows(after_self) + product(z_rows(gelu_f_low), w_mat(9))).astype(bf_type)
+    block_rows = block_rows.reshape(2, z_share // 2, model_width)
 
     pair_width = 2 * own_width
     n_cols = n_dp * pair_width
@@ -607,12 +1060,12 @@
     wanted = ((wanted // pair_width) * n_z + z_rank) * pair_width + wanted % pair_width
     select = (lax.iota(jnp.int32, model_width)[:, None] == wanted[None, :]).astype(bf_type)
 
+    def col_sum(values):
+        return jnp.sum(values, 0)
+
     def chosen(values):
         return product(values, select).astype(bf_type)
 
-    def chosen_sum(values):
-        total_cols = jnp.sum(values, 0).reshape(n_dp, n_z, pair_width)
-        return lax.dynamic_index_in_dim(total_cols, z_rank, 1, keepdims=False).reshape(n_cols)
 
     grad_out = own_of(cotangent).astype(fl_type)
     grad_nine = own_of(cotangent)
@@ -622,7 +1075,7 @@
     grad_up_f = pull_gelu_f(product_nt(grad_nine, w_mat(9)))[0].astype(bf_type)
     terms[8] = product_tn(chosen(norm_f), grad_up_f)
     grad_norm_f = product_nt(grad_up_f, w_mat(8))
-    gain_terms[3] = chosen_sum(hat_f * grad_norm_f)
+    gain_terms[3] = col_sum(hat_f * grad_norm_f)
     grad_self = grad_out + pull(hat_f, inv_f, grad_norm_f * gain_rows[3])
     grad_seven = grad_self.astype(bf_type)
     terms[7] = product_tn(chosen(mixed_heads), grad_seven)
@@ -661,79 +1114,65 @@
         + product_nt(grad_k_self, w_mat(5))
         + product_nt(grad_v_self, w_mat(6))
     )
-    gain_terms[2] = chosen_sum(hat_s * grad_norm_s)
+    gain_terms[2] = col_sum(hat_s * grad_norm_s)
     grad_mlp = grad_self + pull(hat_s, inv_s, grad_norm_s * gain_rows[2])
     grad_three = grad_mlp.astype(bf_type)
     terms[3] = product_tn(chosen(gelu_c_low), grad_three)
     grad_up_c = pull_gelu_c(product_nt(grad_three, w_mat(3)))[0].astype(bf_type)
     terms[2] = product_tn(chosen(norm_c), grad_up_c)
     grad_norm_c = product_nt(grad_up_c, w_mat(2))
-    gain_terms[1] = chosen_sum(hat_c * grad_norm_c)
+    gain_terms[1] = col_sum(hat_c * grad_norm_c)
     grad_cross = grad_mlp + pull(hat_c, inv_c, grad_norm_c * gain_rows[1])
     grad_one = grad_cross.astype(bf_type)
     terms[1] = product_tn(chosen(att_low), grad_one)
     grad_att = product_nt(grad_one, w_mat(1)).astype(bf_type)
     gk_own = product(grad_att, kt_one).astype(bf_type)
     dot_own = jnp.sum(gk_own.astype(fl_type) * mixed_pix, -1)
+    gk_own = jnp.pad(gk_own, ((0, 0), (0, pad_width - pix_width)))
     term_k_one = product_tn(chosen(grad_att), mixed_low)
-
-    early = jnp.stack([terms[index] for index in range(1, 10)])
-    early = early.reshape(9, n_dp * 2, own_width, model_width).swapaxes(0, 1)
-    early = early.reshape(n_dp * 2 * 9 * own_width, model_width).astype(bf_type)
-    early_sum = lax.psum_scatter(early, ("dp", "core"), scatter_dimension=0, tiled=True)
-    early_grad = early_sum.astype(fl_type).reshape(9, own_width, model_width)
-
-    hat_pix, inv_pix = standard_parts(pixels.astype(fl_type))
-    stats_own = jnp.stack([peak, total, dot_own])
-    stats = by_item(stats_own, swap(stats_own))
-    gk_both = by_item(gk_own, swap(gk_own))
-    probs = exp_low.astype(fl_type) * (jnp.exp(peak_loc - stats[:, 0]) / stats[:, 1])[:, None, :]
-    grad_probs = jnp.einsum("ipc,iqc->ipq", norm_pix, gk_both, preferred_element_type=fl_type)
-    grad_scores = (probs * (grad_probs - stats[:, 2][:, None, :])).astype(bf_type)
-    probs_low = probs.astype(bf_type)
-    query_part = jnp.einsum("ipq,ipc->iqc", grad_scores, norm_pix, preferred_element_type=fl_type)
-    query_own = own_of(query_part) + swap(other_of(query_part))
-    query_sum = lax.psum(query_own, "z")
-    grad_norm_p = jnp.einsum(
-        "ipq,iqc->ipc", grad_scores, qk_both, preferred_element_type=fl_type
-    ) + jnp.einsum("ipq,iqc->ipc", probs_low, gk_both, preferred_element_type=fl_type)
-    input_part = jnp.sum(hat_pix * grad_norm_p, (0, 1))
-    pixel_grad = pull(hat_pix, inv_pix, grad_norm_p * input_gain)
-
-    query_low = query_sum.astype(bf_type)
-    grad_query = (product_nt(query_low, kt_zero) * cross_scale).astype(bf_type)
-    term_zero = product_tn(chosen(norm_a), grad_query)
-    grad_norm_a = product_nt(grad_query, w_zero)
-    gain_terms[0] = chosen_sum(hat_a * grad_norm_a)
-    latent_grad = exchange_rows(
-        z_rows(grad_cross)
-        + pull(z_rows(hat_a), z_rows(inv_a), z_rows(grad_norm_a) * gain_rows[0])
-    )
-    term_k_zero = product_tn(chosen(q_own), query_low) * cross_scale
-    gains_cols = jnp.stack([gain_terms[index] for index in range(4)], axis=1)
-    late = jnp.concatenate(
-        [
-            term_zero,
-            jnp.pad(term_k_zero, ((0, 0), (0, pad_width - pix_width))),
+    term_k_one = jnp.pad(term_k_one, ((0, 0), (0, pad_width - pix_width)))
+
+    wire = bf_type if own_width % 16 == 0 else fl_type
+    early = jnp.stack([terms[index] for index in range(1, 10)]).astype(wire)
+    early = early.reshape(9, n_dp, 2, own_width, model_width).transpose(1, 2, 0, 3, 4)
+    early = early.reshape(n_dp, 2, 9 * own_width, model_width)
+    stats_own = jnp.broadcast_to(
+        jnp.stack([peak, total, dot_own])[:, None, :], (3, 8, lat_len)
+    )
+    gain_sums = jnp.stack([gain_terms[index] for index in range(1, 4)])
+    gain_sums = jnp.pad(gain_sums, ((1, 4), (0, 0)))
+    block_out, latent_grad, pixel_grad, wide_grad, kv_grad, gains_grad, small = backward_call(
+        n_z,
+        n_dp,
+        (
+            gk_own,
+            stats_own,
+            early,
+            block_rows,
+            xn,
+            exp_low,
+            peak_loc,
+            qk_both,
+            pixels,
+            input_gain.reshape(1, pix_width),
+            latents,
+            first_all,
+            gain_rows,
+            q_own,
+            z_rows(grad_cross),
             term_k_one,
-            gains_cols,
-            jnp.zeros((n_cols, pad_width - pix_width - 4), fl_type),
-        ],
-        axis=1,
-    ).astype(bf_type)
-    late_sum = lax.psum_scatter(late, ("dp", "core"), scatter_dimension=0, tiled=True).astype(
-        fl_type
-    )
-    wide_grad = jnp.concatenate([late_sum[None, :, :model_width], early_grad], axis=0)
-    kv_grad = jnp.stack(
-        [
-            late_sum[:, model_width : model_width + pix_width].T,
-            late_sum[:, model_width + pad_width : model_width + pad_width + pix_width].T,
-        ]
-    )
-    gains_grad = late_sum[
-        :, model_width + pad_width + pix_width : model_width + pad_width + pix_width + 4
-    ].T
+            gain_sums,
+            weight_mats,
+            mats_first,
+            mats_second,
+            kv_weights,
+            kv_first,
+            kv_second,
+            norm_gains,
+            gains_first,
+            gains_second,
+        ),
+    )
 
     mats_first_new, mats_second_new, mats_update, mats_wsum, mats_usum = moments(
         weight_mats, wide_grad, mats_first, mats_second, (1, 2)
@@ -744,11 +1183,7 @@
     gains_first_new, gains_second_new, gains_update, gains_wsum, gains_usum = moments(
         norm_gains, gains_grad, gains_first, gains_second, (1,)
     )
-    small = jnp.concatenate(
-        [mats_wsum, kv_wsum, gains_wsum, mats_usum, kv_usum, gains_usum, input_part]
-    )
-    small = lax.psum(small, ALL)
-    square_w, square_u, input_grad = small[:16], small[16:32], small[32:]
+    square_w, square_u, input_grad = small[0, :16], small[1, :16], small[2, :pix_width]
     trust = jnp.sqrt(square_w) / (jnp.sqrt(square_u) + 1e-06)
     mats_new = weight_mats - step_rate * trust[0:10, None, None] * mats_update
     kv_new = kv_weights - step_rate * trust[10:12, None, None] * kv_update

time: 497 us -> 381 us (0.77)
  blocking collectives: 76.8 us -> 0 us
  Pallas kernels: 118 us -> 182 us
  waiting for transfers between devices: 54.2 us -> 0 us
  matrix products: 147 us -> 123 us
  between operations: 17 us -> 3.32 us
  other arithmetic: 31.2 us -> 21.1 us
    psum x2 -> x0, blocking collectives: 76.8 us -> none  [the longest x1 39.3 us: local(): small = lax.psum(small, ALL)]
    pallas_call x0 -> x1, Pallas kernels: none -> 64.3 us  [backward_call(): pl.pallas_call(functools.partial(backward, n_z, n_dp, pix_width, chunk),...]
    reduce_scatter x1 -> x0, waiting for transfers between devices: 53.7 us -> none  [local(): lax.psum_scatter(early, ('dp', 'core'), scatter_dimension=0, tiled=True)]
    dot_general x4 -> x0, matrix products: 11.2 us -> none  [the longest x1 5.09 us: local(): jnp.einsum('ipc,iqc->ipq', norm_pix, gk_both, preferred_element_type=fl_t...]
    unnamed x159 -> x118, local copies, waits for them, and re-layouts: 19.4 us -> 28 us
    another operation x14 -> x1, local copies, waits for them, and re-layouts: 6.7 us -> 0.1 us
    dot_general x12 -> x10, matrix products: 30.6 us -> 24 us  [product_tn(): lax.dot_general(left_side, right_side, (((0,), (0,)), ((), ())), preferre...]
    reduce_sum x4 -> x1, other arithmetic: 6.77 us -> 1.19 us  [moments(): jnp.sum(update * update, sum_axes)]
  transfers between devices with their start and end apart: 7 -> 0, of which waited for: 2 -> 0; matrix products, arithmetic and copies ran while one was open for 14% -> 0% of each run, Pallas kernels for 0% -> 0%
where the time goes in v3:
time: 381 us; the launch traced here: 375 us
  Pallas kernels  182 us (48%)
  matrix products  123 us (32%)
  local copies, waits for them, and re-layouts  46.6 us (12%)
  other arithmetic  21.1 us (6%)
    pallas_call x1, Pallas kernels, forward_call(): pl.pallas_call(functools.partial(pixels_forward, n_z, gathers, pix_width,...  118 us
    pallas_call x1, Pallas kernels, backward_call(): pl.pallas_call(functools.partial(backward, n_z, n_dp, pix_width, chunk),...  64.3 us
    dot_general x10, matrix products, product_nt(): lax.dot_general(left_side, right_side, (((1,), (1,)), ((), ())), preferre...  39.3 us
    dot_general x12, matrix products, product(): return jnp.dot(left_side, right_side, preferred_element_type=fl_type)  35.4 us
    unnamed x118, local copies, waits for them, and re-layouts  28 us
    dot_general x10, matrix products, product_tn(): lax.dot_general(left_side, right_side, (((0,), (0,)), ((), ())), preferre...  24 us

profile of v3, /device:TPU:0, one launch (start us, length us, event | category | flops | bytes accessed | tf_op | source)
XLA Modules:
  0.0 375.5 jit_solution(3236941176009387494)
XLA Ops:
  10.9 4.3 %copy.70.refs_1_.refs_8_ = bf16[2,1568,261]{2,1,0:T(8,128)(2,1)} copy(bf16[2,1568,261]{1,0,2:T(2,128)(2,1)S(1)} %copy-done.25) | data formatting | bytes 3273984 | tf_op args[1]
  15.1 117.7 %pixels_forward.1 = (bf16[1024,1792]{1,0:T(8,128)(2,1)}, bf16[9,1024,1024]{2,1,0:T(8,128)(2,1)}, bf16[2,1568,384]{2,1,0:T(8,128)(2,1)}, bf16[2,1568,512]{2,1,0:T...) custom-call(s32[2]{0:T(128)} %counts.1, ...), custom_call_target="tpu_custom_call" | custom-call | tf_op jit(solution)/shard_map/pixels_forward/pallas_call | solution.py:416
  144.9 3.9 %fusion.192 = (f32[512]{0:T(512)S(1)}, f32[512,1024]{1,0:T(8,128)S(1)}) fusion(f32[512,1024]{1,0:T(8,128)S(1)} %get-tuple-element.122, bf16[9,1024,1024]{2,1,0:T(8,128)(2,1)} %get-tuple-element.36, f32[512,1024]{1,0:T(8,128)S(1)} %fusion.45), kind=kOutput, calls=%fused_computation.254 | convolution fusion | flops 1079508480 | bytes 8390656 | tf_op jit(solution)/shard_map/dot_general | solution.py:922
  150.0 3.8 %fusion.112 = bf16[64,8,8,128]{3,2,1,0:T(8,128)(2,1)} fusion(bf16[512,1024]{1,0:T(8,128)(2,1)S(1)} %multiply_convert_fusion.5, bf16[9,1024,1024]{2,1,0:T(8,128)(2,1)} %get-tuple-element.36), kind=kOutput, calls=%fused_computation.122 | convolution fusion | flops 1074266112 | bytes 4194304 | tf_op jit(solution)/shard_map/dot_general | solution.py:922
  153.8 3.8 %fusion.100 = bf16[512,1024]{1,0:T(8,128)(2,1)} fusion(bf16[512,1024]{1,0:T(8,128)(2,1)S(1)} %multiply_convert_fusion.5, bf16[9,1024,1024]{2,1,0:T(8,128)(2,1)} %get-tuple-element.36), kind=kOutput, calls=%fused_computation.119 | convolution fusion | flops 1074266112 | bytes 4194304 | tf_op jit(solution)/shard_map/dot_general | solution.py:922
  157.6 3.8 %fusion.97 = bf16[512,1024]{1,0:T(8,128)(2,1)} fusion(bf16[512,1024]{1,0:T(8,128)(2,1)S(1)} %multiply_convert_fusion.5, bf16[9,1024,1024]{2,1,0:T(8,128)(2,1)} %get-tuple-element.36), kind=kOutput, calls=%fused_computation.118 | convolution fusion | flops 1074266112 | bytes 4194304 | tf_op jit(solution)/shard_map/dot_general | solution.py:922
  166.0 7.4 %fusion.193 = (f32[8,512]{1,0:T(8,128)S(1)}, f32[8,512,512]{1,2,0:T(8,128)}) fusion(bf16[512,8,128]{0,2,1:T(8,128)(2,1)S(1)} %bitcast.225, bf16[512,8,128]{0,2,1:T(8,128)(2,1)} %bitcast.227), kind=kOutput, calls=%fused_computation.255 | convolution fusion | flops 543162880 | bytes 10502144 | tf_op jit(solution)/shard_map/sub | solution.py:917
  173.4 4.6 %fusion.85 = bf16[8,128,512]{2,1,0:T(8,128)(2,1)S(1)} fusion(bf16[64,8,8,128]{3,2,1,0:T(8,128)(2,1)} %fusion.112, f32[8,512,512]{1,2,0:T(8,128)} %get-tuple-element.126, f32[8,512]{1,0:T(8,128)S(1)} %get-tuple-element.125), kind=kOutput, calls=%fused_computation.114 | convolution fusion | flops 541589504 | bytes 10502144 | tf_op jit(solution)/shard_map/hqk,khd->qhd/dot_general | solution.py:1040
  181.4 3.8 %multiply_convert_fusion.1 = (bf16[512,1024]{1,0:T(8,128)(2,1)S(1)}, f32[512,1024]{1,0:T(8,128)S(1)}) fusion(bf16[9,1024,1024]{2,1,0:T(8,128)(2,1)} %get-tuple-element.36, f32[512,1024]{1,0:T(8,128)S(1)} %get-tuple-element.128, f32[1024]{0:T(1024)S(1)} %bitcast.252, f32[512]{0:T(512)S(1)} %add_rsqrt_fusion, f32[512]{0:T(512)S(1)} %broadcast_multiply_fusion.6), kind=kOutput, calls=%fused_computation.66 | convolution fusion | flops 1080557568 | bytes 7348224 | tf_op jit(solution)/shard_map/dot_general | solution.py:922
  185.2 5.0 %fusion.18 = bf16[512,1024]{1,0:T(8,128)(2,1)} fusion(f32[512,1024]{1,0:T(8,128)S(1)} %get-tuple-element.137, bf16[9,1024,1024]{2,1,0:T(8,128)(2,1)} %get-tuple-element.36, bf16[2,512,1024]{2,1,0:T(8,128)(2,1)S(1)} %copy-done.31, s32[]{:T(128)S(6)} %select_n.31), kind=kOutput, calls=%fused_computation.25 | convolution fusion | flops 1084227584 | bytes 6291460 | tf_op jit(solution)/shard_map/dot_general | solution.py:932
  194.1 4.0 %convolution_convert_fusion.2 = bf16[256,1024]{1,0:T(8,128)(2,1)} fusion(bf16[512,1024]{1,0:T(8,128)(2,1)} %fusion.18, s32[256]{0:T(256)S(1)} %fusion.180, f32[512,1024]{1,0:T(8,128)} %copy-done.9, f32[1024]{0:T(1024)S(1)} %bitcast.253, f32[512]{0:T(512)S(1)} %add_rsqrt_fusion, f32[512]{0:T(512)S(1)} %broadcast_multiply_fusion.6), kind=kOutput, calls=%fused_computation.127 | convolution fusion | flops 539623424 | bytes 3679232 | tf_op jit(solution)/shard_map/dot_general | solution.py:926
  198.1 4.4 %multiply_reduce_fusion.2 = (f32[1024]{0:T(1024)S(1)}, f32[512]{0:T(512)S(1)}, f32[512]{0:T(512)S(1)}, f32[512,1024]{1,0:T(8,128)S(1)}) fusion(f32[512,1024]{1,0:T(8,128)} %copy-done.9, f32[512]{0:T(512)S(1)} %add_rsqrt_fusion, f32[512]{0:T(512)S(1)} %broadcast_multiply_fusion.6, f32[1024]{0:T(1024)S(1)} %bitcast.254, bf16[512,1024]{1,0:T(8,128)(2,1)} %fusion.18, ...), kind=kOutput, calls=%fused_computation.63 | convolution fusion | flops 1077934080 | bytes 7356416 | tf_op jit(solution)/shard_map/dot_general | solution.py:932
  208.5 4.5 %fusion.103 = bf16[512,1024]{1,0:T(8,128)(2,1)} fusion(bf16[9,1024,1024]{2,1,0:T(8,128)(2,1)} %get-tuple-element.36, f32[512,1024]{1,0:T(8,128)} %multiply_add_fusion.2), kind=kOutput, calls=%fused_computation.120 | convolution fusion | flops 1074790400 | bytes 5242880 | tf_op jit(solution)/shard_map/dot_general | solution.py:932
  214.5 5.0 %fusion.88 = bf16[8,128,512]{2,1,0:T(8,128)(2,1)S(1)} fusion(bf16[512,8,128]{0,2,1:T(8,128)(2,1)S(1)} %bitcast.236, f32[8,512,512]{1,2,0:T(8,128)} %get-tuple-element.126, f32[8,512]{1,0:T(8,128)S(1)} %get-tuple-element.125), kind=kOutput, calls=%fused_computation.115 | convolution fusion | flops 541589504 | bytes 10502144 | tf_op jit(solution)/shard_map/hqk,qhd->khd/dot_general | solution.py:1104
  219.5 4.6 %multiply_reduce_fusion = (f32[8,512]{1,0:T(8,128)S(1)}, f32[8,512,512]{1,2,0:T(8,128)S(1)}) fusion(f32[8,512,512]{1,2,0:T(8,128)} %get-tuple-element.126, f32[8,512]{1,0:T(8,128)S(1)} %get-tuple-element.125, bf16[512,8,128]{0,2,1:T(8,128)(2,1)S(1)} %bitcast.237, bf16[64,8,8,128]{3,2,1,0:T(8,128)(2,1)S(1)} %copy-done.47), kind=kOutput, calls=%fused_computation.2 | convolution fusion | flops 543158272 | bytes 18907136 | tf_op jit(solution)/shard_map/qhd,khd->hqk/dot_general | solution.py:1083
  236.8 3.9 %multiply_reduce_fusion.3 = (f32[1024]{0:T(1024)S(1)}, f32[512]{0:T(512)S(1)}, f32[512]{0:T(512)S(1)}, f32[512,1024]{1,0:T(8,128)S(1)}) fusion(f32[512,1024]{1,0:T(8,128)S(1)} %get-tuple-element.124, f32[512]{0:T(512)S(1)} %add_rsqrt_fusion.1, f32[512]{0:T(512)S(1)} %broadcast_multiply_fusion.7, f32[1024]{0:T(1024)S(1)} %bitcast.245, ...), kind=kOutput, calls=%fused_computation.64 | convolution fusion | flops 1078982656 | bytes 11550720 | tf_op jit(solution)/shard_map/dot_general | solution.py:932
  242.7 4.7 %convolution_convert_fusion.7 = bf16[256,1024]{1,0:T(8,128)(2,1)} fusion(s32[256]{0:T(256)S(1)} %fusion.180, f32[512,1024]{1,0:T(8,128)} %multiply_add_fusion.1, f32[512,1024]{1,0:T(8,128)} %copy-done.46), kind=kOutput, calls=%fused_computation.132 | convolution fusion | flops 542769152 | bytes 4719616 | tf_op jit(solution)/shard_map/dot_general | solution.py:926
  247.4 5.5 %fusion.11 = bf16[512,1024]{1,0:T(8,128)(2,1)} fusion(f32[512,1024]{1,0:T(8,128)} %copy-done.46, bf16[9,1024,1024]{2,1,0:T(8,128)(2,1)} %get-tuple-element.36, f32[512,1024]{1,0:T(8,128)S(1)} %copy-done.4), kind=kOutput, calls=%fused_computation.18 | convolution fusion | flops 1084751872 | bytes 7340032 | tf_op jit(solution)/shard_map/dot_general | solution.py:932
  252.9 4.2 %convolution_convert_fusion.8 = bf16[256,1024]{1,0:T(8,128)(2,1)} fusion(bf16[512,1024]{1,0:T(8,128)(2,1)} %fusion.11, s32[256]{0:T(256)S(1)} %fusion.180, f32[512,1024]{1,0:T(8,128)} %copy-done.6, f32[1024]{0:T(1024)S(1)} %bitcast.249, f32[512]{0:T(512)S(1)} %add_rsqrt_fusion.2, f32[512]{0:T(512)S(1)} %broadcast_multiply_fusion.8), kind=kOutput, calls=%fused_computation.133 | convolution fusion | flops 539623424 | bytes 3679232 | tf_op jit(solution)/shard_map/dot_general | solution.py:926
  257.1 4.0 %multiply_reduce_fusion.4 = (f32[1024]{0:T(1024)S(1)}, f32[512]{0:T(512)S(1)}, f32[512]{0:T(512)S(1)}, f32[512,1024]{1,0:T(8,128)S(1)}) fusion(f32[512,1024]{1,0:T(8,128)S(1)} %copy-done.7, f32[512]{0:T(512)S(1)} %add_rsqrt_fusion.2, f32[512]{0:T(512)S(1)} %broadcast_multiply_fusion.8, f32[1024]{0:T(1024)S(1)} %bitcast.250, bf16[512,1024]{1,0:T(8,128)(2,1)} %fusion.11, ...), kind=kOutput, calls=%fused_computation.65 | convolution fusion | flops 1077934080 | bytes 7356416 | tf_op jit(solution)/shard_map/dot_general | solution.py:932
  261.8 3.8 %fusion.91 = bf16[512,1024]{1,0:T(8,128)(2,1)} fusion(bf16[9,1024,1024]{2,1,0:T(8,128)(2,1)} %get-tuple-element.36, f32[512,1024]{1,0:T(8,128)S(1)} %multiply_add_fusion), kind=kOutput, calls=%fused_computation.116 | convolution fusion | flops 1074790400 | bytes 5242880 | tf_op jit(solution)/shard_map/dot_general | solution.py:932
  283.5 64.3 %backward.1 = (bf16[2,64,1024]{2,1,0:T(8,128)(2,1)}, f32[2,64,1024]{2,1,0:T(8,128)}, f32[2,1568,261]{2,1,0:T(8,128)}, f32[10,32,1024]{2,1,0:T(8,128)}, f32[2,261...) custom-call(bf16[512,384]{1,0:T(8,128)(2,1)} %pad.24.refs_0_, f32[3,8,512]{2,1,0:T(8,128)} %broadcast_in_dim.5.refs_1_, ...), custom_call_target="tpu_custom_call" | custom-call | tf_op jit(solution)/shard_map/backward/pallas_call | solution.py:886
  360.5 4.5 %multiply_subtract_fusion = (f32[10,32,1024]{2,1,0:T(8,128)}, f32[10,32,1024]{2,1,0:T(8,128)}, f32[10,32,1024]{2,1,0:T(8,128)}) fusion(f32[10,32,1024]{2,1,0:T(8,128)S(1)} %copy-done.2, f32[10]{0:T(128)S(1)} %multiply_bitcast_fusion.2, f32[10,32,1024]{2,1,0:T(8,128)} %get-tuple-element.162, f32[10,32,1024]{2,1,0:T(8,128)S(1)} %copy-done.11, ...), kind=kLoop, calls=%fused_computation.124 | loop fusion | flops 4915200 | bytes 9175080 | tf_op jit(solution)/shard_map/sub | solution.py:1188
  365.0 6.9 %copy.99 = f32[2,1568,261]{1,0,2:T(2,128)} copy(f32[2,1568,261]{2,1,0:T(8,128)} %get-tuple-element.74) | data formatting | bytes 6547968
  (190 shorter events, 89.8 us)
Async XLA Ops:
  0.7 8.5 %copy-start.1 = (f32[10,32,1024]{2,1,0:T(8,128)S(1)}, f32[10,32,1024]{2,1,0:T(8,128)}, u32[]{:S(2)}) copy-start(f32[10,32,1024]{2,1,0:T(8,128)} %refs_17_.1) | copy-start | bytes 3932164
  5.5 5.4 %copy-start.25 = (bf16[2,1568,261]{1,0,2:T(2,128)(2,1)S(1)}, bf16[2,1568,261]{1,0,2:T(2,128)(2,1)}, u32[]{:S(2)}) copy-start(bf16[2,1568,261]{1,0,2:T(2,128)(2,1)} %param.17) | copy-start | bytes 4910980
  135.8 5.4 %copy-start.34 = (bf16[320,512]{0,1:T(8,128)(2,1)}, bf16[320,512]{0,1:T(8,128)(2,1)S(1)}, u32[]{:S(2)}) copy-start(bf16[320,512]{0,1:T(8,128)(2,1)S(1)} %copy.71) | copy-start | bytes 983044
  162.9 10.5 %copy-start.15 = (bf16[512,1024]{0,1:T(8,128)(2,1)}, bf16[512,1024]{0,1:T(8,128)(2,1)S(1)}, u32[]{:S(2)}) copy-start(bf16[512,1024]{0,1:T(8,128)(2,1)S(1)} %copy.117) | copy-start | bytes 3145732
  181.0 9.2 %copy-start.9 = (f32[512,1024]{1,0:T(8,128)}, f32[512,1024]{1,0:T(8,128)S(1)}, u32[]{:S(2)}) copy-start(f32[512,1024]{1,0:T(8,128)S(1)} %get-tuple-element.128) | copy-start | bytes 6291460
  214.5 5.0 %copy-start.47 = (bf16[64,8,8,128]{3,2,1,0:T(8,128)(2,1)S(1)}, bf16[64,8,8,128]{3,2,1,0:T(8,128)(2,1)}, u32[]{:S(2)}) copy-start(bf16[64,8,8,128]{3,2,1,0:T(8,128)(2,1)} %fusion.112) | copy-start | bytes 3145732
  219.5 17.3 %copy-start.18 = (bf16[8,128,512]{2,1,0:T(8,128)(2,1)}, bf16[8,128,512]{2,1,0:T(8,128)(2,1)S(1)}, u32[]{:S(2)}) copy-start(bf16[8,128,512]{2,1,0:T(8,128)(2,1)S(1)} %fusion.88) | copy-start | bytes 3145732
  219.5 5.0 %slice-start = ((s8[8388608]{0:T(1024)(128)(4,1)}), s8[4194304]{0:T(1024)(128)(4,1)S(1)}, s32[]{:S(2)}) async-start(s8[8388608]{0:T(1024)(128)(4,1)} %bitcast.218), calls=%async_computation | async-start | bytes 8388608
  219.5 6.3 %slice-start.1 = ((s8[8388608]{0:T(1024)(128)(4,1)}), s8[4194304]{0:T(1024)(128)(4,1)S(1)}, s32[]{:S(2)}) async-start(s8[8388608]{0:T(1024)(128)(4,1)} %bitcast.218), calls=%async_computation.1 | async-start | bytes 8388608
  283.5 66.2 %copy-start.20 = (f32[2,261,32]{2,1,0:T(8,128)S(1)}, f32[2,261,32]{2,1,0:T(8,128)}, u32[]{:S(2)}) copy-start(f32[2,261,32]{2,1,0:T(8,128)} %copy.92.refs_21_) | copy-start | bytes 200452
  283.5 66.2 %copy-start.21 = (f32[2,261,32]{2,1,0:T(8,128)S(1)}, f32[2,261,32]{2,1,0:T(8,128)}, u32[]{:S(2)}) copy-start(f32[2,261,32]{2,1,0:T(8,128)} %copy.93.refs_22_) | copy-start | bytes 200452
  283.5 66.2 %copy-start.22 = (f32[2,261,32]{2,1,0:T(8,128)S(1)}, f32[2,261,32]{2,1,0:T(8,128)}, u32[]{:S(2)}) copy-start(f32[2,261,32]{2,1,0:T(8,128)} %copy.91.refs_20_) | copy-start | bytes 200452
  347.8 7.2 %copy-start.37 = (f32[4,32]{1,0:T(4,128)S(1)}, f32[4,32]{1,0:T(4,128)}, u32[]{:S(2)}) copy-start(f32[4,32]{1,0:T(4,128)} %refs_23_.1) | copy-start | bytes 1540
  347.8 7.2 %copy-start.39 = (f32[4,32]{1,0:T(4,128)S(1)}, f32[4,32]{1,0:T(4,128)}, u32[]{:S(2)}) copy-start(f32[4,32]{1,0:T(4,128)} %refs_24_.1) | copy-start | bytes 1540
  347.9 7.2 %copy-start.40 = (f32[4,32]{1,0:T(4,128)S(1)}, f32[4,32]{1,0:T(4,128)}, u32[]{:S(2)}) copy-start(f32[4,32]{1,0:T(4,128)} %refs_25_.1) | copy-start | bytes 1540
  347.9 7.2 %copy-start.42 = (f32[4,32]{1,0:T(4,128)S(1)}, f32[4,32]{1,0:T(4,128)}, u32[]{:S(2)}) copy-start(f32[4,32]{1,0:T(4,128)} %get-tuple-element.164) | copy-start | bytes 1540
  347.9 7.8 %copy-start.38 = (f32[261]{0:T(512)S(1)}, f32[261]{0:T(512)}, u32[]{:S(2)}) copy-start(f32[261]{0:T(512)} %param.23) | copy-start | bytes 3136
  347.9 7.8 %copy-start.43 = (f32[261]{0:T(512)S(1)}, f32[261]{0:T(512)}, u32[]{:S(2)}) copy-start(f32[261]{0:T(512)} %param.30) | copy-start | bytes 3136
  347.9 7.8 %copy-start.44 = (f32[261]{0:T(512)S(1)}, f32[261]{0:T(512)}, u32[]{:S(2)}) copy-start(f32[261]{0:T(512)} %param.31) | copy-start | bytes 3136
  347.9 12.6 %copy-start.2 = (f32[10,32,1024]{2,1,0:T(8,128)S(1)}, f32[10,32,1024]{2,1,0:T(8,128)}, u32[]{:S(2)}) copy-start(f32[10,32,1024]{2,1,0:T(8,128)} %refs_17_.1) | copy-start | bytes 3932164
  347.9 12.6 %copy-start.11 = (f32[10,32,1024]{2,1,0:T(8,128)S(1)}, f32[10,32,1024]{2,1,0:T(8,128)}, u32[]{:S(2)}) copy-start(f32[10,32,1024]{2,1,0:T(8,128)} %refs_18_.1) | copy-start | bytes 3932164
  349.5 15.4 %copy-start.41 = (f32[261]{0:T(512)}, f32[261]{0:T(512)S(1)}, u32[]{:S(2)}) copy-start(f32[261]{0:T(512)S(1)} %slice_reduce_fusion) | copy-start | bytes 3136
  365.0 7.0 %copy-start.36 = (bf16[2,64,1024]{2,1,0:T(8,128)(2,1)S(1)}, bf16[2,64,1024]{2,1,0:T(8,128)(2,1)}, u32[]{:S(2)}) copy-start(bf16[2,64,1024]{2,1,0:T(8,128)(2,1)} %get-tuple-element.159) | copy-start | bytes 786436
  365.0 7.7 %copy-start.28 = (f32[2,64,1024]{2,1,0:T(8,128)S(1)}, f32[2,64,1024]{2,1,0:T(8,128)}, u32[]{:S(2)}) copy-start(f32[2,64,1024]{2,1,0:T(8,128)} %get-tuple-element.160) | copy-start | bytes 1572868
  (26 other events, 78.9 us)
